TPU v7x, 256 devices: a whole 4x4x8 slice. The times are simulated.
256 devices in a mesh: len: 8 (over x, core), wid: 32 (over y, z).
Axes of the slice: x: 4, y: 4, z: 8, core: 2. Of those that a mesh axis runs over, the one named last changes fastest.
Arguments:
- velocity: float32 [2, 256, 1024, 256], P(None, 'len', 'wid'), may hold values from -6 to 6
- bfield: float32 [256, 1024, 256], P('len', 'wid'), may hold values from 0.5 to 1.5
- material: int32 [256, 1024, 256], P('len', 'wid'), may hold values from 0 to 2
- wall_mask: int32 [256, 1024, 256], P('len', 'wid'), may hold values 0 or 1
- potential_guess: float32 [256, 1024, 256], P('len', 'wid'), may hold values from -6 to 6
Outputs:
- new_velocity: float32 [2, 256, 1024, 256], P(None, 'len', 'wid')
- potential: float32 [256, 1024, 256], P('len', 'wid')
All inputs are finite; a program needn't handle non-finite values. No bound on the sum of `wall_mask` on one device may be relied on, other than what follows from the above.
Results may differ from a plain program's by a relative error of at most 0.000026.
Values sent between devices are 32-bit elements; how exact they have to be, the bound alone decides.
A program may use at most 64 MiB of HBM per device.

v0:
```python
import jax
import jax.numpy as jnp
from jax import lax
from jax.sharding import PartitionSpec as P

SWEEPS = 4


CONTACT_GAIN = 2.0
TIME_STEP = 0.5
LOWER_BOUND = 0.1
UPPER_BOUND = 2.0
CENTRE_VALUE = 0.5 * (UPPER_BOUND + LOWER_BOUND)
HALF_SPREAD = 0.5 * (UPPER_BOUND - LOWER_BOUND)
RATIO_ONE = CENTRE_VALUE / HALF_SPREAD


def padded(cells, sides, width):
    for axis, dim in sides:
        count = lax.axis_size(axis)
        ends = count - 1
        head = lax.slice_in_dim(cells, 0, width, axis=dim)
        tail = lax.slice_in_dim(cells, cells.shape[dim] - width, cells.shape[dim], axis=dim)
        cells = jnp.concatenate(
            [
                lax.ppermute(tail, axis, [(i, (i + 1) % count) for i in range(ends)]),
                cells,
                lax.ppermute(head, axis, [((i + 1) % count, i) for i in range(ends)]),
            ],
            axis=dim,
        )
    return cells


def offset_view(field, i, j):
    rows = field.shape[0] - 2
    cols = field.shape[1] - 2
    return field[1 + i : 1 + i + rows, 1 + j : 1 + j + cols]


def trim_margin(field, margin_from, margin_to):
    cut = margin_from - margin_to
    if cut == 0:
        return field
    return field[cut : field.shape[0] - cut, cut : field.shape[1] - cut]


def inside_mask(rows_dev, cols_dev, extra):
    len_places = (
        jnp.arange(rows_dev + 2 * extra, dtype=jnp.int32) - extra + lax.axis_index("len") * rows_dev
    )
    len_valid = ((len_places >= 0) & (len_places < rows_dev * lax.axis_size("len"))).astype(
        jnp.float32
    )
    wid_places = (
        jnp.arange(cols_dev + 2 * extra, dtype=jnp.int32) - extra + lax.axis_index("wid") * cols_dev
    )
    wid_valid = ((wid_places >= 0) & (wid_places < cols_dev * lax.axis_size("wid"))).astype(
        jnp.float32
    )
    return len_valid[:, None, None] * wid_valid[None, :, None]


def upward(field):
    return jnp.concatenate([field[:, :, 1:], jnp.zeros_like(field[:, :, :1])], axis=2)


def downward(field):
    return jnp.concatenate([jnp.zeros_like(field[:, :, :1]), field[:, :, :-1]], axis=2)


def conductivity(material):
    melt = (material == 0).astype(jnp.float32)
    shell = (material == 1).astype(jnp.float32)
    copper = (material == 2).astype(jnp.float32)
    return 1.0 * melt + 0.5 * shell + 6.0 * copper


def operate(field, conduct, contact):
    centre = offset_view(field, 0, 0)
    own_cond = offset_view(conduct, 0, 0)
    summed = CONTACT_GAIN * contact * centre
    for i, j in ((1, 0), (-1, 0), (0, 1), (0, -1)):
        summed = summed + 0.5 * (own_cond + offset_view(conduct, i, j)) * (
            centre - offset_view(field, i, j)
        )
    summed = summed + 0.5 * (own_cond + upward(own_cond)) * (centre - upward(centre))
    summed = summed + 0.5 * (own_cond + downward(own_cond)) * (centre - downward(centre))
    return summed


def diagonal_of(conduct, contact):
    own_cond = offset_view(conduct, 0, 0)
    summed = CONTACT_GAIN * contact
    for i, j in ((1, 0), (-1, 0), (0, 1), (0, -1)):
        summed = summed + 0.5 * (own_cond + offset_view(conduct, i, j))
    summed = summed + 0.5 * (own_cond + upward(own_cond))
    summed = summed + 0.5 * (own_cond + downward(own_cond))
    return summed


def source_of(conduct, field_len, field_wid):
    own_cond = offset_view(conduct, 0, 0)
    len_centre = offset_view(field_len, 0, 0)
    wid_centre = offset_view(field_wid, 0, 0)
    summed = -(0.5 * (own_cond + offset_view(conduct, 1, 0))) * (
        0.5 * (len_centre + offset_view(field_len, 1, 0))
    )
    summed = summed + 0.5 * (own_cond + offset_view(conduct, -1, 0)) * (
        0.5 * (len_centre + offset_view(field_len, -1, 0))
    )
    summed = summed - 0.5 * (own_cond + offset_view(conduct, 0, 1)) * (
        0.5 * (wid_centre + offset_view(field_wid, 0, 1))
    )
    summed = summed + 0.5 * (own_cond + offset_view(conduct, 0, -1)) * (
        0.5 * (wid_centre + offset_view(field_wid, 0, -1))
    )
    return summed


def body(velocity, bfield, material, wall_mask, potential_guess):
    conduct = conductivity(material)
    contact = wall_mask.astype(jnp.float32)
    rows_dev = conduct.shape[0]
    cols_dev = conduct.shape[1]
    field_len = velocity[1] * bfield
    field_wid = -velocity[0] * bfield
    margin = 1
    stacked = jnp.stack([conduct, field_len, field_wid, contact, potential_guess])
    widened = padded(stacked, (("len", 1), ("wid", 2)), 1)
    cond_wide = widened[0]
    len_wide = widened[1]
    wid_wide = widened[2]
    contact_wide = widened[3]
    guess_wide = widened[4]
    contact_inner = trim_margin(contact_wide, margin, margin - 1)
    source = source_of(cond_wide, len_wide, wid_wide)
    diagonal = diagonal_of(cond_wide, contact_inner)
    residual = source - operate(guess_wide, cond_wide, contact_inner)
    direction = (
        residual / diagonal * (1.0 / CENTRE_VALUE) * inside_mask(rows_dev, cols_dev, margin - 1)
    )
    potential = trim_margin(guess_wide, margin, 0)
    margin_res = margin - 1
    margin_dir = margin - 1
    weight_now = 1.0 / RATIO_ONE
    for sweep in range(SWEEPS):
        potential = potential + trim_margin(direction, margin_dir, 0)
        if sweep < SWEEPS - 1:
            direction = padded(direction, (("len", 0), ("wid", 1)), 1)
            margin_dir = 1
            image = operate(
                direction,
                trim_margin(cond_wide, margin, margin_dir),
                trim_margin(contact_wide, margin, margin_dir - 1),
            )
            residual = trim_margin(residual, margin_res, margin_dir - 1) - image
            weight_next = 1.0 / (2.0 * RATIO_ONE - weight_now)
            keep_factor = weight_next * weight_now
            new_factor = 2.0 * weight_next / HALF_SPREAD
            direction = keep_factor * trim_margin(
                direction, margin_dir, margin_dir - 1
            ) + new_factor * (residual / trim_margin(diagonal, margin - 1, margin_dir - 1))
            direction = direction * inside_mask(rows_dev, cols_dev, margin_dir - 1)
            weight_now = weight_next
            margin_res = margin_dir - 1
            margin_dir = margin_dir - 1
    pot_pad = padded(potential, (("len", 0), ("wid", 1)), 1)
    grad_len = 0.5 * (offset_view(pot_pad, 1, 0) - offset_view(pot_pad, -1, 0))
    grad_wid = 0.5 * (offset_view(pot_pad, 0, 1) - offset_view(pot_pad, 0, -1))
    current_len = conduct * (field_len - grad_len)
    current_wid = conduct * (field_wid - grad_wid)
    new_len = velocity[0] + TIME_STEP * current_wid * bfield
    new_wid = velocity[1] - TIME_STEP * current_len * bfield
    return (jnp.stack([new_len, new_wid]), potential)


def solution(mesh):
    placed = (
        P(None, "len", "wid", None),
        P("len", "wid", None),
        P("len", "wid", None),
        P("len", "wid", None),
        P("len", "wid", None),
    )
    return jax.shard_map(
        body,
        mesh=mesh,
        in_specs=placed,
        out_specs=(P(None, "len", "wid", None), P("len", "wid", None)),
        check_vma=False,
    )
```

profile of v0, /device:TPU:27, one launch (start us, length us, event | category | flops | bytes accessed | tf_op | source)
XLA Modules:
  0.0 126.6 jit_solution(8451510915279358428)
XLA Ops:
  0.6 0.0 copy-start.3
  0.6 0.0 copy-start.4
  0.7 1.6 %bitcast_dynamic-update-slice_fusion.4 = f32[5,32,32,256]{3,2,1,0:T(8,128)S(1)} fusion(s32[32,32,256]{2,1,0:T(8,128)} %param.7), kind=kLoop, calls=%fused_computation.145 | loop fusion | flops 2097151 | bytes 2097152
  2.3 1.9 %bitcast_dynamic-update-slice_fusion.3 = f32[5,32,32,256]{3,2,1,0:T(8,128)S(1)} fusion(f32[5,32,32,256]{3,2,1,0:T(8,128)S(1)} %bitcast_dynamic-update-slice_fusion.4, f32[32,32,256]{2,1,0:T(8,128)} %param.6, f32[2,32,32,256]{3,2,1,0:T(8,128)} %param.5), kind=kLoop, calls=%fused_computation.143 | loop fusion | flops 262144 | bytes 3145728
  4.2 0.2 bitcast_dynamic-update-slice_fusion.2
  4.4 0.1 bitcast_dynamic-update-slice_fusion.1
  4.5 0.1 bitcast_dynamic-update-slice_fusion
  4.7 2.3 %copy-done = f32[5,32,32,256]{3,2,1,0:T(8,128)} copy-done((f32[5,32,32,256]{3,2,1,0:T(8,128)}, f32[5,32,32,256]{3,2,1,0:T(8,128)S(1)}, u32[]{:S(2)}) %copy-start) | copy-done | bytes 5242904
  7.0 0.8 fusion.96
  7.7 3.7 %collective-permute-start = (f32[5,1,32,256]{3,2,1,0:T(8,128)}, f32[5,1,32,256]{3,2,1,0:T(8,128)S(1)}, u32[]{:S(2)}, u32[]{:S(2)}) collective-permute-start(f32[5,1,32,256]{3,2,1,0:T(8,128)} %get-tuple-element.24), channel_id=1, source_target_pairs={{0,32},{32,64},{64,96},{96,128},{128,160},{160,192},{192,224},{1,3... | collective-permute-start | bytes 491528 | tf_op jit(solution)/shard_map/ppermute | solution.py:26
  11.4 1.9 %collective-permute-start.1 = (f32[5,1,32,256]{3,2,1,0:T(8,128)}, f32[5,1,32,256]{3,2,1,0:T(8,128)S(1)}, u32[]{:S(2)}, u32[]{:S(2)}) collective-permute-start(f32[5,1,32,256]{3,2,1,0:T(8,128)} %get-tuple-element.25), channel_id=1, source_target_pairs={{32,0},{64,32},{96,64},{128,96},{160,128},{192,160},{224,192},{33,... | collective-permute-start | bytes 491528 | tf_op jit(solution)/shard_map/ppermute | solution.py:28
  13.4 0.6 collective-permute-done
  14.0 4.3 %collective-permute-done.1 = f32[5,1,32,256]{3,2,1,0:T(8,128)S(1)} collective-permute-done((f32[5,1,32,256]{3,2,1,0:T(8,128)}, f32[5,1,32,256]{3,2,1,0:T(8,128)S(1)}, u32[]{:S(2)}, u32[]{:S(2)}) %collective-permute-start.1) | collective-permute-done | bytes 163872 | tf_op jit(solution)/shard_map/ppermute | solution.py:28
  18.3 2.0 %pad_maximum_fusion.36 = (f32[5,34,1,256]{3,2,1,0:T(1,128)S(1)}, f32[5,34,1,256]{3,2,1,0:T(1,128)S(1)}) fusion(f32[5,1,32,256]{3,2,1,0:T(8,128)S(1)} %collective-permute-done.1, f32[5,32,32,256]{3,2,1,0:T(8,128)} %copy-done, f32[5,1,32,256]{3,2,1,0:T(8,128)S(1)} %collective-permute-done), kind=kLoop, calls=%fused_computation.158 | loop fusion | flops 174080 | bytes 5918720 | tf_op jit(solution)/shard_map/slice | solution.py:23
  20.3 3.5 %collective-permute-start.2 = (f32[5,34,1,256]{3,2,1,0:T(1,128)S(1)}, f32[5,34,1,256]{3,2,1,0:T(1,128)S(1)}, u32[]{:S(2)}, u32[]{:S(2)}) collective-permute-start(f32[5,34,1,256]{3,2,1,0:T(1,128)S(1)} %get-tuple-element.20), channel_id=1, source_target_pairs={{0,1},{1,2},{2,3},{3,4},{4,5},{5,6},{6,7},{7,8},{8,9},{9,10},{10,1... | collective-permute-start | bytes 522248 | tf_op jit(solution)/shard_map/ppermute | solution.py:26
  23.8 6.0 %collective-permute-start.3 = (f32[5,34,1,256]{3,2,1,0:T(1,128)S(1)}, f32[5,34,1,256]{3,2,1,0:T(1,128)S(1)}, u32[]{:S(2)}, u32[]{:S(2)}) collective-permute-start(f32[5,34,1,256]{3,2,1,0:T(1,128)S(1)} %get-tuple-element.21), channel_id=1, source_target_pairs={{1,0},{2,1},{3,2},{4,3},{5,4},{6,5},{7,6},{8,7},{9,8},{10,9},{11,1... | collective-permute-start | bytes 522248 | tf_op jit(solution)/shard_map/ppermute | solution.py:28
  29.9 0.1 broadcast_multiply_fusion.1
  29.9 1.7 %collective-permute-done.2 = f32[5,34,1,256]{3,2,1,0:T(1,128)S(1)} collective-permute-done((f32[5,34,1,256]{3,2,1,0:T(1,128)S(1)}, f32[5,34,1,256]{3,2,1,0:T(1,128)S(1)}, u32[]{:S(2)}, u32[]{:S(2)}) %collective-permute-start.2) | collective-permute-done | bytes 174112 | tf_op jit(solution)/shard_map/ppermute | solution.py:26
  31.6 1.8 %collective-permute-done.3 = f32[5,34,1,256]{3,2,1,0:T(1,128)S(1)} collective-permute-done((f32[5,34,1,256]{3,2,1,0:T(1,128)S(1)}, f32[5,34,1,256]{3,2,1,0:T(1,128)S(1)}, u32[]{:S(2)}, u32[]{:S(2)}) %collective-permute-start.3) | collective-permute-done | bytes 174112 | tf_op jit(solution)/shard_map/ppermute | solution.py:28
  33.4 1.3 %pad_maximum_fusion = f32[5,34,34,256]{3,2,1,0:T(8,128)S(1)} fusion(f32[5,34,1,256]{3,2,1,0:T(1,128)S(1)} %collective-permute-done.3, f32[5,1,32,256]{3,2,1,0:T(8,128)S(1)} %collective-permute-done.1, f32[5,32,32,256]{3,2,1,0:T(8,128)S(1)} %copy-done.1, f32[5,1,32,256]{3,2,1,0:T(8,128)S(1)} %collective-permute-done, f32[5,34,1,256]{3,2,1,0:T(1,128)S(1)} %collective-permute-done.2), kind=kLoop, calls=%fused_computation | loop fusion | flops 5918720 | bytes 11837440 | tf_op jit(solution)/shard_map/concatenate | solution.py:24
  34.7 0.5 slice_bitcast_fusion.3
  35.2 2.4 %fusion.97 = (f32[32,32,255]{2,1,0:T(8,128)S(1)}, f32[32,32,255]{2,1,0:T(8,128)}, f32[32,32,255]{2,1,0:T(8,128)}, f32[32,32,255]{2,1,0:T(8,128)}) fusion(f32[34,34,256]{2,1,0:T(8,128)S(1)} %get-tuple-element.15, f32[34,34,256]{2,1,0:T(8,128)S(1)} %get-tuple-element.19), kind=kLoop, calls=%fused_computation.176 | loop fusion | bytes 8355840 | tf_op jit(solution)/shard_map/slice | solution.py:69
  37.6 5.4 %divide_multiply_fusion = (f32[32,32,256]{2,1,0:T(8,128)S(1)}, f32[32,32,256]{2,1,0:T(8,128)S(1)}, f32[32,32,256]{2,1,0:T(8,128)S(1)}, f32[32,32,256]{2,1,0:T(8,...) fusion(f32[32,32]{1,0:T(8,128)S(1)} %get-tuple-element.53, ...), kind=kLoop, calls=%fused_computation.151 | loop fusion | flops 14942208 | bytes 31444992 | tf_op jit(solution)/shard_map/mul | solution.py:141
  43.0 3.1 %collective-permute-start.5 = (f32[1,32,256]{2,1,0:T(8,128)S(1)}, f32[1,32,256]{2,1,0:T(8,128)S(1)}, u32[]{:S(2)}, u32[]{:S(2)}) collective-permute-start(f32[1,32,256]{2,1,0:T(8,128)S(1)} %get-tuple-element.48), channel_id=1, source_target_pairs={{0,32},{32,64},{64,96},{96,128},{128,160},{160,192},{192,224},{1,3... | collective-permute-start | bytes 98312 | tf_op jit(solution)/shard_map/ppermute | solution.py:26
  46.1 1.9 %collective-permute-start.4 = (f32[1,32,256]{2,1,0:T(8,128)S(1)}, f32[1,32,256]{2,1,0:T(8,128)S(1)}, u32[]{:S(2)}, u32[]{:S(2)}) collective-permute-start(f32[1,32,256]{2,1,0:T(8,128)S(1)} %get-tuple-element.49), channel_id=1, source_target_pairs={{32,0},{64,32},{96,64},{128,96},{160,128},{192,160},{224,192},{33,... | collective-permute-start | bytes 98312 | tf_op jit(solution)/shard_map/ppermute | solution.py:28
  48.0 3.3 %collective-permute-done.4 = f32[1,32,256]{2,1,0:T(8,128)S(1)} collective-permute-done((f32[1,32,256]{2,1,0:T(8,128)S(1)}, f32[1,32,256]{2,1,0:T(8,128)S(1)}, u32[]{:S(2)}, u32[]{:S(2)}) %collective-permute-start.4) | collective-permute-done | bytes 32800 | tf_op jit(solution)/shard_map/ppermute | solution.py:28
  51.3 0.1 pad_maximum_fusion.48
  51.4 6.2 %collective-permute-start.6 = (f32[34,1,256]{2,1,0:T(1,128)S(1)}, f32[34,1,256]{2,1,0:T(1,128)S(1)}, u32[]{:S(2)}, u32[]{:S(2)}) collective-permute-start(f32[34,1,256]{2,1,0:T(1,128)S(1)} %get-tuple-element.36), channel_id=1, source_target_pairs={{1,0},{2,1},{3,2},{4,3},{5,4},{6,5},{7,6},{8,7},{9,8},{10,9},{11,1... | collective-permute-start | bytes 104456 | tf_op jit(solution)/shard_map/ppermute | solution.py:28
  57.6 1.9 %collective-permute-start.7 = (f32[34,1,256]{2,1,0:T(1,128)S(1)}, f32[34,1,256]{2,1,0:T(1,128)S(1)}, u32[]{:S(2)}, u32[]{:S(2)}) collective-permute-start(f32[34,1,256]{2,1,0:T(1,128)S(1)} %get-tuple-element.37), channel_id=1, source_target_pairs={{0,1},{1,2},{2,3},{3,4},{4,5},{5,6},{6,7},{7,8},{8,9},{9,10},{10,1... | collective-permute-start | bytes 104456 | tf_op jit(solution)/shard_map/ppermute | solution.py:26
  59.5 0.4 fusion.105
  59.9 0.0 collective-permute-done.6
  59.9 4.5 %collective-permute-done.7 = f32[34,1,256]{2,1,0:T(1,128)S(1)} collective-permute-done((f32[34,1,256]{2,1,0:T(1,128)S(1)}, f32[34,1,256]{2,1,0:T(1,128)S(1)}, u32[]{:S(2)}, u32[]{:S(2)}) %collective-permute-start.7) | collective-permute-done | bytes 34848 | tf_op jit(solution)/shard_map/ppermute | solution.py:26
  64.4 3.0 %add_multiply_fusion.1 = (f32[32,32,256]{2,1,0:T(8,128)S(1)}, f32[32,32,256]{2,1,0:T(8,128)S(1)}) fusion(f32[32,32,256]{2,1,0:T(8,128)S(1)} %get-tuple-element.7, f32[32,32]{1,0:T(8,128)S(1)} %get-tuple-element.52, f32[32,32,256]{2,1,0:T(8,128)S(1)} %get-tuple-element.8, f32[32,32]{1,0:T(8,128)S(1)} %get-tuple-element.53, ...), kind=kLoop, calls=%fused_computation.150 | loop fusion | flops 9437184 | bytes 14815232 | tf_op jit(solution)/shard_map/mul | solution.py:164
  67.4 3.3 %collective-permute-start.9 = (f32[1,32,256]{2,1,0:T(8,128)S(1)}, f32[1,32,256]{2,1,0:T(8,128)S(1)}, u32[]{:S(2)}, u32[]{:S(2)}) collective-permute-start(f32[1,32,256]{2,1,0:T(8,128)S(1)} %get-tuple-element.44), channel_id=1, source_target_pairs={{0,32},{32,64},{64,96},{96,128},{128,160},{160,192},{192,224},{1,3... | collective-permute-start | bytes 98312 | tf_op jit(solution)/shard_map/ppermute | solution.py:26
  70.7 1.9 %collective-permute-start.8 = (f32[1,32,256]{2,1,0:T(8,128)S(1)}, f32[1,32,256]{2,1,0:T(8,128)S(1)}, u32[]{:S(2)}, u32[]{:S(2)}) collective-permute-start(f32[1,32,256]{2,1,0:T(8,128)S(1)} %get-tuple-element.45), channel_id=1, source_target_pairs={{32,0},{64,32},{96,64},{128,96},{160,128},{192,160},{224,192},{33,... | collective-permute-start | bytes 98312 | tf_op jit(solution)/shard_map/ppermute | solution.py:28
  72.7 0.0 collective-permute-done.9
  72.7 3.3 %collective-permute-done.8 = f32[1,32,256]{2,1,0:T(8,128)S(1)} collective-permute-done((f32[1,32,256]{2,1,0:T(8,128)S(1)}, f32[1,32,256]{2,1,0:T(8,128)S(1)}, u32[]{:S(2)}, u32[]{:S(2)}) %collective-permute-start.8) | collective-permute-done | bytes 32800 | tf_op jit(solution)/shard_map/ppermute | solution.py:28
  76.0 0.1 pad_maximum_fusion.45
  76.0 1.9 %collective-permute-start.10 = (f32[34,1,256]{2,1,0:T(1,128)S(1)}, f32[34,1,256]{2,1,0:T(1,128)S(1)}, u32[]{:S(2)}, u32[]{:S(2)}) collective-permute-start(f32[34,1,256]{2,1,0:T(1,128)S(1)} %get-tuple-element.34), channel_id=1, source_target_pairs={{1,0},{2,1},{3,2},{4,3},{5,4},{6,5},{7,6},{8,7},{9,8},{10,9},{11,1... | collective-permute-start | bytes 104456 | tf_op jit(solution)/shard_map/ppermute | solution.py:28
  78.0 3.4 %collective-permute-start.11 = (f32[34,1,256]{2,1,0:T(1,128)S(1)}, f32[34,1,256]{2,1,0:T(1,128)S(1)}, u32[]{:S(2)}, u32[]{:S(2)}) collective-permute-start(f32[34,1,256]{2,1,0:T(1,128)S(1)} %get-tuple-element.35), channel_id=1, source_target_pairs={{0,1},{1,2},{2,3},{3,4},{4,5},{5,6},{6,7},{7,8},{8,9},{9,10},{10,1... | collective-permute-start | bytes 104456 | tf_op jit(solution)/shard_map/ppermute | solution.py:26
  81.3 0.4 fusion.103
  81.7 3.0 %collective-permute-done.11 = f32[34,1,256]{2,1,0:T(1,128)S(1)} collective-permute-done((f32[34,1,256]{2,1,0:T(1,128)S(1)}, f32[34,1,256]{2,1,0:T(1,128)S(1)}, u32[]{:S(2)}, u32[]{:S(2)}) %collective-permute-start.11) | collective-permute-done | bytes 34848 | tf_op jit(solution)/shard_map/ppermute | solution.py:26
  84.7 3.1 %add_multiply_fusion = (f32[32,32,256]{2,1,0:T(8,128)S(1)}, f32[32,32,256]{2,1,0:T(8,128)S(1)}) fusion(f32[32,32,256]{2,1,0:T(8,128)S(1)} %get-tuple-element.7, f32[32,32]{1,0:T(8,128)S(1)} %get-tuple-element.52, f32[32,32,256]{2,1,0:T(8,128)S(1)} %get-tuple-element.5, f32[32,32,256]{2,1,0:T(8,128)S(1)} %get-tuple-element.8, ...), kind=kLoop, calls=%fused_computation.149 | loop fusion | flops 10747904 | bytes 15863808 | tf_op jit(solution)/shard_map/mul | solution.py:164
  87.9 3.1 %collective-permute-start.13 = (f32[1,32,256]{2,1,0:T(8,128)S(1)}, f32[1,32,256]{2,1,0:T(8,128)S(1)}, u32[]{:S(2)}, u32[]{:S(2)}) collective-permute-start(f32[1,32,256]{2,1,0:T(8,128)S(1)} %get-tuple-element.40), channel_id=1, source_target_pairs={{0,32},{32,64},{64,96},{96,128},{128,160},{160,192},{192,224},{1,3... | collective-permute-start | bytes 98312 | tf_op jit(solution)/shard_map/ppermute | solution.py:26
  90.9 1.9 %collective-permute-start.12 = (f32[1,32,256]{2,1,0:T(8,128)S(1)}, f32[1,32,256]{2,1,0:T(8,128)S(1)}, u32[]{:S(2)}, u32[]{:S(2)}) collective-permute-start(f32[1,32,256]{2,1,0:T(8,128)S(1)} %get-tuple-element.41), channel_id=1, source_target_pairs={{32,0},{64,32},{96,64},{128,96},{160,128},{192,160},{224,192},{33,... | collective-permute-start | bytes 98312 | tf_op jit(solution)/shard_map/ppermute | solution.py:28
  92.9 0.0 collective-permute-done.13
  92.9 3.3 %collective-permute-done.12 = f32[1,32,256]{2,1,0:T(8,128)S(1)} collective-permute-done((f32[1,32,256]{2,1,0:T(8,128)S(1)}, f32[1,32,256]{2,1,0:T(8,128)S(1)}, u32[]{:S(2)}, u32[]{:S(2)}) %collective-permute-start.12) | collective-permute-done | bytes 32800 | tf_op jit(solution)/shard_map/ppermute | solution.py:28
  96.2 0.1 pad_maximum_fusion.42
  96.2 1.9 %collective-permute-start.14 = (f32[34,1,256]{2,1,0:T(1,128)S(1)}, f32[34,1,256]{2,1,0:T(1,128)S(1)}, u32[]{:S(2)}, u32[]{:S(2)}) collective-permute-start(f32[34,1,256]{2,1,0:T(1,128)S(1)} %get-tuple-element.32), channel_id=1, source_target_pairs={{1,0},{2,1},{3,2},{4,3},{5,4},{6,5},{7,6},{8,7},{9,8},{10,9},{11,1... | collective-permute-start | bytes 104456 | tf_op jit(solution)/shard_map/ppermute | solution.py:28
  98.1 3.4 %collective-permute-start.15 = (f32[34,1,256]{2,1,0:T(1,128)S(1)}, f32[34,1,256]{2,1,0:T(1,128)S(1)}, u32[]{:S(2)}, u32[]{:S(2)}) collective-permute-start(f32[34,1,256]{2,1,0:T(1,128)S(1)} %get-tuple-element.33), channel_id=1, source_target_pairs={{0,1},{1,2},{2,3},{3,4},{4,5},{5,6},{6,7},{7,8},{8,9},{9,10},{10,1... | collective-permute-start | bytes 104456 | tf_op jit(solution)/shard_map/ppermute | solution.py:26
  101.5 0.4 fusion.101
  101.9 3.0 %collective-permute-done.15 = f32[34,1,256]{2,1,0:T(1,128)S(1)} collective-permute-done((f32[34,1,256]{2,1,0:T(1,128)S(1)}, f32[34,1,256]{2,1,0:T(1,128)S(1)}, u32[]{:S(2)}, u32[]{:S(2)}) %collective-permute-start.15) | collective-permute-done | bytes 34848 | tf_op jit(solution)/shard_map/ppermute | solution.py:26
  104.9 3.3 %multiply_add_fusion = f32[32,32,256]{2,1,0:T(8,128)S(1)} fusion(f32[32,32,256]{2,1,0:T(8,128)S(1)} %get-tuple-element.2, f32[32,32,256]{2,1,0:T(8,128)S(1)} %get-tuple-element.7, f32[32,32,256]{2,1,0:T(8,128)S(1)} %get-tuple-element.3, f32[32,32,256]{2,1,0:T(8,128)S(1)} %get-tuple-element.10, f32[32,32,255]{2,1,0:T(8,128)S(1)} %get-tuple-element.43, ...), kind=kLoop, calls=%fused_computation.148 | loop fusion | flops 11796480 | bytes 16912384 | tf_op jit(solution)/shard_map/add | solution.py:148
  108.3 0.0 copy-start.2
  108.3 1.9 %collective-permute-start.17 = (f32[1,32,256]{2,1,0:T(8,128)S(1)}, f32[1,32,256]{2,1,0:T(8,128)S(1)}, u32[]{:S(2)}, u32[]{:S(2)}) collective-permute-start(f32[1,32,256]{2,1,0:T(8,128)S(1)} %get-tuple-element.38), channel_id=1, source_target_pairs={{32,0},{64,32},{96,64},{128,96},{160,128},{192,160},{224,192},{33,... | collective-permute-start | bytes 98312 | tf_op jit(solution)/shard_map/ppermute | solution.py:28
  110.2 3.6 %collective-permute-start.16 = (f32[1,32,256]{2,1,0:T(8,128)S(1)}, f32[1,32,256]{2,1,0:T(8,128)S(1)}, u32[]{:S(2)}, u32[]{:S(2)}) collective-permute-start(f32[1,32,256]{2,1,0:T(8,128)S(1)} %get-tuple-element.39), channel_id=1, source_target_pairs={{0,32},{32,64},{64,96},{96,128},{128,160},{160,192},{192,224},{1,3... | collective-permute-start | bytes 98312 | tf_op jit(solution)/shard_map/ppermute | solution.py:26
  113.9 0.0 collective-permute-done.17
  113.9 1.0 collective-permute-done.16
  114.9 0.1 pad_maximum_fusion.39
  115.0 1.9 %collective-permute-start.18 = (f32[34,1,256]{2,1,0:T(1,128)S(1)}, f32[34,1,256]{2,1,0:T(1,128)S(1)}, u32[]{:S(2)}, u32[]{:S(2)}) collective-permute-start(f32[34,1,256]{2,1,0:T(1,128)S(1)} %get-tuple-element.30), channel_id=1, source_target_pairs={{1,0},{2,1},{3,2},{4,3},{5,4},{6,5},{7,6},{8,7},{9,8},{10,9},{11,1... | collective-permute-start | bytes 104456 | tf_op jit(solution)/shard_map/ppermute | solution.py:28
  116.9 3.4 %collective-permute-start.19 = (f32[34,1,256]{2,1,0:T(1,128)S(1)}, f32[34,1,256]{2,1,0:T(1,128)S(1)}, u32[]{:S(2)}, u32[]{:S(2)}) collective-permute-start(f32[34,1,256]{2,1,0:T(1,128)S(1)} %get-tuple-element.31), channel_id=1, source_target_pairs={{0,1},{1,2},{2,3},{3,4},{4,5},{5,6},{6,7},{7,8},{8,9},{9,10},{10,1... | collective-permute-start | bytes 104456 | tf_op jit(solution)/shard_map/ppermute | solution.py:26
  120.3 3.4 %collective-permute-done.19 = f32[34,1,256]{2,1,0:T(1,128)S(1)} collective-permute-done((f32[34,1,256]{2,1,0:T(1,128)S(1)}, f32[34,1,256]{2,1,0:T(1,128)S(1)}, u32[]{:S(2)}, u32[]{:S(2)}) %collective-permute-start.19) | collective-permute-done | bytes 34848 | tf_op jit(solution)/shard_map/ppermute | solution.py:26
  123.7 1.3 %fusion.15 = (f32[1,32,32,256]{3,2,1,0:T(8,128)S(1)}, f32[1,32,32,256]{3,2,1,0:T(8,128)S(1)}) fusion(f32[32,32,256]{2,1,0:T(8,128)S(1)} %copy-done.3, f32[34,1,256]{2,1,0:T(1,128)S(1)} %collective-permute-done.19, f32[1,32,256]{2,1,0:T(8,128)S(1)} %collective-permute-done.17, f32[32,32,256]{2,1,0:T(8,128)S(1)} %multiply_add_fusion, ...), kind=kLoop, calls=%fused_computation.25 | loop fusion | flops 8650752 | bytes 7475200 | tf_op jit(solution)/shard_map/stack | solution.py:175
  125.0 1.6 %pad_maximum_fusion.1 = f32[2,32,32,256]{3,2,1,0:T(8,128)} fusion(f32[1,32,32,256]{3,2,1,0:T(8,128)S(1)} %get-tuple-element.23, f32[1,32,32,256]{3,2,1,0:T(8,128)S(1)} %get-tuple-element.22), kind=kLoop, calls=%fused_computation.1 | loop fusion | flops 524288 | bytes 4194304 | tf_op jit(solution)/shard_map/stack | solution.py:175
  (21 shorter events, 0.1 us)
Async XLA Ops:
  0.6 3.6 %copy-start.3 = (f32[32,32,256]{2,1,0:T(8,128)S(1)}, f32[32,32,256]{2,1,0:T(8,128)}, u32[]{:S(2)}) copy-start(f32[32,32,256]{2,1,0:T(8,128)} %param.6) | copy-start | bytes 3145732
  0.6 3.6 %copy-start.4 = (f32[2,32,32,256]{3,2,1,0:T(8,128)S(1)}, f32[2,32,32,256]{3,2,1,0:T(8,128)}, u32[]{:S(2)}) copy-start(f32[2,32,32,256]{3,2,1,0:T(8,128)} %param.5) | copy-start | bytes 6291460
  0.7 3.8 %copy-start.6 = (s32[32,32,256]{2,1,0:T(8,128)S(1)}, s32[32,32,256]{2,1,0:T(8,128)}, u32[]{:S(2)}) copy-start(s32[32,32,256]{2,1,0:T(8,128)} %param.8) | copy-start | bytes 3145732
  0.7 3.9 %copy-start.7 = (f32[32,32,256]{2,1,0:T(8,128)S(1)}, f32[32,32,256]{2,1,0:T(8,128)}, u32[]{:S(2)}) copy-start(f32[32,32,256]{2,1,0:T(8,128)} %param.9) | copy-start | bytes 3145732
  4.7 2.3 %copy-start = (f32[5,32,32,256]{3,2,1,0:T(8,128)}, f32[5,32,32,256]{3,2,1,0:T(8,128)S(1)}, u32[]{:S(2)}) copy-start(f32[5,32,32,256]{3,2,1,0:T(8,128)S(1)} %bitcast_dynamic-update-slice_fusion) | copy-start | bytes 15728644
  7.7 6.2 %collective-permute-start = (f32[5,1,32,256]{3,2,1,0:T(8,128)}, f32[5,1,32,256]{3,2,1,0:T(8,128)S(1)}, u32[]{:S(2)}, u32[]{:S(2)}) collective-permute-start(f32[5,1,32,256]{3,2,1,0:T(8,128)} %get-tuple-element.24), channel_id=1, source_target_pairs={{0,32},{32,64},{64,96},{96,128},{128,160},{160,192},{192,224},{1,3... | collective-permute-start | bytes 491528 | tf_op jit(solution)/shard_map/ppermute | solution.py:26
  11.4 6.8 %collective-permute-start.1 = (f32[5,1,32,256]{3,2,1,0:T(8,128)}, f32[5,1,32,256]{3,2,1,0:T(8,128)S(1)}, u32[]{:S(2)}, u32[]{:S(2)}) collective-permute-start(f32[5,1,32,256]{3,2,1,0:T(8,128)} %get-tuple-element.25), channel_id=1, source_target_pairs={{32,0},{64,32},{96,64},{128,96},{160,128},{192,160},{224,192},{33,... | collective-permute-start | bytes 491528 | tf_op jit(solution)/shard_map/ppermute | solution.py:28
  13.4 20.0 %copy-start.1 = (f32[5,32,32,256]{3,2,1,0:T(8,128)S(1)}, f32[5,32,32,256]{3,2,1,0:T(8,128)}, u32[]{:S(2)}) copy-start(f32[5,32,32,256]{3,2,1,0:T(8,128)} %copy-done) | copy-start | bytes 15728644
  20.3 11.4 %collective-permute-start.2 = (f32[5,34,1,256]{3,2,1,0:T(1,128)S(1)}, f32[5,34,1,256]{3,2,1,0:T(1,128)S(1)}, u32[]{:S(2)}, u32[]{:S(2)}) collective-permute-start(f32[5,34,1,256]{3,2,1,0:T(1,128)S(1)} %get-tuple-element.20), channel_id=1, source_target_pairs={{0,1},{1,2},{2,3},{3,4},{4,5},{5,6},{6,7},{7,8},{8,9},{9,10},{10,1... | collective-permute-start | bytes 522248 | tf_op jit(solution)/shard_map/ppermute | solution.py:26
  23.8 9.6 %collective-permute-start.3 = (f32[5,34,1,256]{3,2,1,0:T(1,128)S(1)}, f32[5,34,1,256]{3,2,1,0:T(1,128)S(1)}, u32[]{:S(2)}, u32[]{:S(2)}) collective-permute-start(f32[5,34,1,256]{3,2,1,0:T(1,128)S(1)} %get-tuple-element.21), channel_id=1, source_target_pairs={{1,0},{2,1},{3,2},{4,3},{5,4},{6,5},{7,6},{8,7},{9,8},{10,9},{11,1... | collective-permute-start | bytes 522248 | tf_op jit(solution)/shard_map/ppermute | solution.py:28
  43.0 5.0 %collective-permute-start.5 = (f32[1,32,256]{2,1,0:T(8,128)S(1)}, f32[1,32,256]{2,1,0:T(8,128)S(1)}, u32[]{:S(2)}, u32[]{:S(2)}) collective-permute-start(f32[1,32,256]{2,1,0:T(8,128)S(1)} %get-tuple-element.48), channel_id=1, source_target_pairs={{0,32},{32,64},{64,96},{96,128},{128,160},{160,192},{192,224},{1,3... | collective-permute-start | bytes 98312 | tf_op jit(solution)/shard_map/ppermute | solution.py:26
  46.1 5.2 %collective-permute-start.4 = (f32[1,32,256]{2,1,0:T(8,128)S(1)}, f32[1,32,256]{2,1,0:T(8,128)S(1)}, u32[]{:S(2)}, u32[]{:S(2)}) collective-permute-start(f32[1,32,256]{2,1,0:T(8,128)S(1)} %get-tuple-element.49), channel_id=1, source_target_pairs={{32,0},{64,32},{96,64},{128,96},{160,128},{192,160},{224,192},{33,... | collective-permute-start | bytes 98312 | tf_op jit(solution)/shard_map/ppermute | solution.py:28
  51.4 8.5 %collective-permute-start.6 = (f32[34,1,256]{2,1,0:T(1,128)S(1)}, f32[34,1,256]{2,1,0:T(1,128)S(1)}, u32[]{:S(2)}, u32[]{:S(2)}) collective-permute-start(f32[34,1,256]{2,1,0:T(1,128)S(1)} %get-tuple-element.36), channel_id=1, source_target_pairs={{1,0},{2,1},{3,2},{4,3},{5,4},{6,5},{7,6},{8,7},{9,8},{10,9},{11,1... | collective-permute-start | bytes 104456 | tf_op jit(solution)/shard_map/ppermute | solution.py:28
  57.6 6.8 %collective-permute-start.7 = (f32[34,1,256]{2,1,0:T(1,128)S(1)}, f32[34,1,256]{2,1,0:T(1,128)S(1)}, u32[]{:S(2)}, u32[]{:S(2)}) collective-permute-start(f32[34,1,256]{2,1,0:T(1,128)S(1)} %get-tuple-element.37), channel_id=1, source_target_pairs={{0,1},{1,2},{2,3},{3,4},{4,5},{5,6},{6,7},{7,8},{8,9},{9,10},{10,1... | collective-permute-start | bytes 104456 | tf_op jit(solution)/shard_map/ppermute | solution.py:26
  67.4 5.3 %collective-permute-start.9 = (f32[1,32,256]{2,1,0:T(8,128)S(1)}, f32[1,32,256]{2,1,0:T(8,128)S(1)}, u32[]{:S(2)}, u32[]{:S(2)}) collective-permute-start(f32[1,32,256]{2,1,0:T(8,128)S(1)} %get-tuple-element.44), channel_id=1, source_target_pairs={{0,32},{32,64},{64,96},{96,128},{128,160},{160,192},{192,224},{1,3... | collective-permute-start | bytes 98312 | tf_op jit(solution)/shard_map/ppermute | solution.py:26
  70.7 5.2 %collective-permute-start.8 = (f32[1,32,256]{2,1,0:T(8,128)S(1)}, f32[1,32,256]{2,1,0:T(8,128)S(1)}, u32[]{:S(2)}, u32[]{:S(2)}) collective-permute-start(f32[1,32,256]{2,1,0:T(8,128)S(1)} %get-tuple-element.45), channel_id=1, source_target_pairs={{32,0},{64,32},{96,64},{128,96},{160,128},{192,160},{224,192},{33,... | collective-permute-start | bytes 98312 | tf_op jit(solution)/shard_map/ppermute | solution.py:28
  76.0 5.7 %collective-permute-start.10 = (f32[34,1,256]{2,1,0:T(1,128)S(1)}, f32[34,1,256]{2,1,0:T(1,128)S(1)}, u32[]{:S(2)}, u32[]{:S(2)}) collective-permute-start(f32[34,1,256]{2,1,0:T(1,128)S(1)} %get-tuple-element.34), channel_id=1, source_target_pairs={{1,0},{2,1},{3,2},{4,3},{5,4},{6,5},{7,6},{8,7},{9,8},{10,9},{11,1... | collective-permute-start | bytes 104456 | tf_op jit(solution)/shard_map/ppermute | solution.py:28
  78.0 6.8 %collective-permute-start.11 = (f32[34,1,256]{2,1,0:T(1,128)S(1)}, f32[34,1,256]{2,1,0:T(1,128)S(1)}, u32[]{:S(2)}, u32[]{:S(2)}) collective-permute-start(f32[34,1,256]{2,1,0:T(1,128)S(1)} %get-tuple-element.35), channel_id=1, source_target_pairs={{0,1},{1,2},{2,3},{3,4},{4,5},{5,6},{6,7},{7,8},{8,9},{9,10},{10,1... | collective-permute-start | bytes 104456 | tf_op jit(solution)/shard_map/ppermute | solution.py:26
  87.9 5.0 %collective-permute-start.13 = (f32[1,32,256]{2,1,0:T(8,128)S(1)}, f32[1,32,256]{2,1,0:T(8,128)S(1)}, u32[]{:S(2)}, u32[]{:S(2)}) collective-permute-start(f32[1,32,256]{2,1,0:T(8,128)S(1)} %get-tuple-element.40), channel_id=1, source_target_pairs={{0,32},{32,64},{64,96},{96,128},{128,160},{160,192},{192,224},{1,3... | collective-permute-start | bytes 98312 | tf_op jit(solution)/shard_map/ppermute | solution.py:26
  90.9 5.2 %collective-permute-start.12 = (f32[1,32,256]{2,1,0:T(8,128)S(1)}, f32[1,32,256]{2,1,0:T(8,128)S(1)}, u32[]{:S(2)}, u32[]{:S(2)}) collective-permute-start(f32[1,32,256]{2,1,0:T(8,128)S(1)} %get-tuple-element.41), channel_id=1, source_target_pairs={{32,0},{64,32},{96,64},{128,96},{160,128},{192,160},{224,192},{33,... | collective-permute-start | bytes 98312 | tf_op jit(solution)/shard_map/ppermute | solution.py:28
  96.2 5.7 %collective-permute-start.14 = (f32[34,1,256]{2,1,0:T(1,128)S(1)}, f32[34,1,256]{2,1,0:T(1,128)S(1)}, u32[]{:S(2)}, u32[]{:S(2)}) collective-permute-start(f32[34,1,256]{2,1,0:T(1,128)S(1)} %get-tuple-element.32), channel_id=1, source_target_pairs={{1,0},{2,1},{3,2},{4,3},{5,4},{6,5},{7,6},{8,7},{9,8},{10,9},{11,1... | collective-permute-start | bytes 104456 | tf_op jit(solution)/shard_map/ppermute | solution.py:28
  98.1 6.8 %collective-permute-start.15 = (f32[34,1,256]{2,1,0:T(1,128)S(1)}, f32[34,1,256]{2,1,0:T(1,128)S(1)}, u32[]{:S(2)}, u32[]{:S(2)}) collective-permute-start(f32[34,1,256]{2,1,0:T(1,128)S(1)} %get-tuple-element.33), channel_id=1, source_target_pairs={{0,1},{1,2},{2,3},{3,4},{4,5},{5,6},{6,7},{7,8},{8,9},{9,10},{10,1... | collective-permute-start | bytes 104456 | tf_op jit(solution)/shard_map/ppermute | solution.py:26
  104.9 18.7 %copy-start.5 = (s32[32,32,256]{2,1,0:T(8,128)S(1)}, s32[32,32,256]{2,1,0:T(8,128)}, u32[]{:S(2)}) copy-start(s32[32,32,256]{2,1,0:T(8,128)} %param.7) | copy-start | bytes 3145732
  108.3 18.3 %copy-start.2 = (f32[32,32,256]{2,1,0:T(8,128)}, f32[32,32,256]{2,1,0:T(8,128)S(1)}, u32[]{:S(2)}) copy-start(f32[32,32,256]{2,1,0:T(8,128)S(1)} %multiply_add_fusion) | copy-start | bytes 3145732
  108.3 5.6 %collective-permute-start.17 = (f32[1,32,256]{2,1,0:T(8,128)S(1)}, f32[1,32,256]{2,1,0:T(8,128)S(1)}, u32[]{:S(2)}, u32[]{:S(2)}) collective-permute-start(f32[1,32,256]{2,1,0:T(8,128)S(1)} %get-tuple-element.38), channel_id=1, source_target_pairs={{32,0},{64,32},{96,64},{128,96},{160,128},{192,160},{224,192},{33,... | collective-permute-start | bytes 98312 | tf_op jit(solution)/shard_map/ppermute | solution.py:28
  110.2 4.7 %collective-permute-start.16 = (f32[1,32,256]{2,1,0:T(8,128)S(1)}, f32[1,32,256]{2,1,0:T(8,128)S(1)}, u32[]{:S(2)}, u32[]{:S(2)}) collective-permute-start(f32[1,32,256]{2,1,0:T(8,128)S(1)} %get-tuple-element.39), channel_id=1, source_target_pairs={{0,32},{32,64},{64,96},{96,128},{128,160},{160,192},{192,224},{1,3... | collective-permute-start | bytes 98312 | tf_op jit(solution)/shard_map/ppermute | solution.py:26
  115.0 5.3 %collective-permute-start.18 = (f32[34,1,256]{2,1,0:T(1,128)S(1)}, f32[34,1,256]{2,1,0:T(1,128)S(1)}, u32[]{:S(2)}, u32[]{:S(2)}) collective-permute-start(f32[34,1,256]{2,1,0:T(1,128)S(1)} %get-tuple-element.30), channel_id=1, source_target_pairs={{1,0},{2,1},{3,2},{4,3},{5,4},{6,5},{7,6},{8,7},{9,8},{10,9},{11,1... | collective-permute-start | bytes 104456 | tf_op jit(solution)/shard_map/ppermute | solution.py:28
  116.9 6.8 %collective-permute-start.19 = (f32[34,1,256]{2,1,0:T(1,128)S(1)}, f32[34,1,256]{2,1,0:T(1,128)S(1)}, u32[]{:S(2)}, u32[]{:S(2)}) collective-permute-start(f32[34,1,256]{2,1,0:T(1,128)S(1)} %get-tuple-element.31), channel_id=1, source_target_pairs={{0,1},{1,2},{2,3},{3,4},{4,5},{5,6},{6,7},{7,8},{8,9},{9,10},{10,1... | collective-permute-start | bytes 104456 | tf_op jit(solution)/shard_map/ppermute | solution.py:26
where the time goes:
time: 129 us; the launch traced here: 127 us
  starting transfers between devices  60 us (47%)
  waiting for transfers between devices  33.2 us (26%)
  other arithmetic  25.1 us (19%)
  local copies, waits for them, and re-layouts  7.23 us (6%)
    ppermute x10, starting transfers between devices, padded(): lax.ppermute(tail, axis, [(i, (i + 1) % count) for i in range(ends)])  32.4 us
    ppermute x10, starting transfers between devices, padded(): lax.ppermute(head, axis, [((i + 1) % count, i) for i in range(ends)])  27.6 us
    ppermute x10, waiting for transfers between devices, padded(): lax.ppermute(tail, axis, [(i, (i + 1) % count) for i in range(ends)])  17.3 us
    ppermute x10, waiting for transfers between devices, padded(): lax.ppermute(head, axis, [((i + 1) % count, i) for i in range(ends)])  15.9 us
    mul x2, other arithmetic, body(): direction = direction * inside_mask(rows_dev, cols_dev, margin_dir - 1)  6.07 us
    mul x1, other arithmetic, body(): residual / diagonal * (1.0 / CENTRE_VALUE)  5.36 us
    unnamed x4, other arithmetic  3.81 us
    add x1, other arithmetic, body(): potential = potential + trim_margin(direction, margin_dir, 0)  3.34 us
  transfers between devices with their start and end apart: 20, of which 12 were waited for; matrix products, arithmetic and copies ran while one was open for 1% of the time, Pallas kernels for 0%

commit v1 on v0

v1 whole, which is shorter than its diff:
```python
import functools

import jax
import jax.numpy as jnp
from jax import lax
from jax.experimental import pallas as pl
from jax.experimental.pallas import tpu as pltpu
from jax.sharding import PartitionSpec as P

MESH = pl.DeviceIdType.MESH
SWEEPS = 4
THETA = 0.5 * (2.0 + 0.1)
DELTA = 0.5 * (2.0 - 0.1)
S1 = THETA / DELTA

ROWS = 32
DEEP = 4
NAT0 = DEEP * 32
PAD = 8
TROWS = 64
TOWN = 16
TAREA = pl.ds(12, 40)
PW = 48
FIRST = (-4, 26)


def chebyshev():
    weight = 1.0 / S1
    gains, alphas, betas = [1.0 / THETA], [], []
    kf_old = nf_old = None
    for _ in range(SWEEPS - 1):
        weight_next = 1.0 / (2.0 * S1 - weight)
        kf, nf = weight_next * weight, 2.0 * weight_next / DELTA
        if nf_old is None:
            alphas.append(kf / nf + THETA - 1.0)
            betas.append(0.0)
        else:
            alphas.append(kf / nf + 1.0 / nf_old - 1.0)
            betas.append(-kf_old / (nf_old * nf_old))
        gains.append(nf * gains[-1])
        kf_old, nf_old, weight = kf, nf, weight_next
    return gains, alphas, betas


GAINS, ALPHAS, BETAS = chebyshev()


def lanes_of(shape):
    return lax.broadcasted_iota(jnp.int32, shape, 1)


def k_up(x, zero):
    r = [pltpu.roll(v, 127, 1) for v in x]
    last = lanes_of(x[0].shape) == 127
    return [jnp.where(last, r[1], r[0]), jnp.where(last, 0.0, r[1]) if zero else r[1]]


def k_down(x, zero):
    r = [pltpu.roll(v, 1, 1) for v in x]
    first = lanes_of(x[0].shape) == 0
    return [jnp.where(first, 0.0, r[0]) if zero else r[0], jnp.where(first, r[0], r[1])]


def kernel(n_len, n_wid, u_hbm, b_hbm, m_hbm, w_hbm, g_hbm, vel_out, pot_out,
           U0, U1, B, MAT, WALL, G, HL, HW, QP, QM, C, K, RP, DP, E0, E1, E2, E3, TN, GH,
           CT, KT, GT, QS, QR, E0T, E1T, E2T, E3T, TT, POT, lsem, ssem, rsem):
    li, wi = lax.axis_index("len"), lax.axis_index("wid")
    has = {(-1, 0): li > 0, (1, 0): li < n_len - 1, (0, -1): wi > 0, (0, 1): wi < n_wid - 1}
    for dl in (-1, 1):
        for dw in (-1, 1):
            has[dl, dw] = jnp.logical_and(has[dl, 0], has[0, dw])
    straight = ((0, -1), (0, 1), (-1, 0), (1, 0))
    diagonal = ((-1, -1), (-1, 1), (1, -1), (1, 1))

    barrier = pltpu.get_barrier_semaphore()
    for way in straight:
        @pl.when(has[way])
        def _():
            pl.semaphore_signal(barrier, inc=1, device_id=(li + way[0], wi + way[1]), device_id_type=MESH)

    own = pl.ds(PAD, 1024)
    loads = []
    for src, dst in (
        (m_hbm, lambda h: MAT.at[h]), (g_hbm, lambda h: G.at[h, own]), (b_hbm, lambda h: B.at[h]),
        (u_hbm.at[0], lambda h: U0.at[h]), (u_hbm.at[1], lambda h: U1.at[h]), (w_hbm, lambda h: WALL.at[h]),
    ):
        for h in range(2):
            copy = pltpu.make_async_copy(src.at[:, pl.ds(128 * h, 128)], dst(h), lsem.at[len(loads)])
            copy.start()
            loads.append(copy)

    for dl in (-1, 1):
        rows = pl.ds(0, 128) if dl < 0 else pl.ds(NAT0 + 1024, 128)
        @pl.when(jnp.logical_not(has[dl, 0]))
        def _():
            for ref in (C, K, E0, QP, QM):
                for h in range(2):
                    ref[h, rows, :] = jnp.zeros((128, 128), jnp.float32)
            for h in range(2):
                GH[(dl + 1) // 2, h] = jnp.zeros((32, 128), jnp.float32)
    for dw in (-1, 1):
        side = (dw + 1) // 2
        c0 = 0 if dw < 0 else 6
        @pl.when(jnp.logical_not(has[0, dw]))
        def _():
            for h in range(2):
                QR[side, h] = jnp.zeros((32, 128), jnp.float32)
                for c in range(c0, c0 + 4):
                    for ref in (CT, KT, GT, E0T):
                        ref[side, c, h, pl.ds(TOWN, 32), :] = jnp.zeros((32, 128), jnp.float32)
    for dl, dw in diagonal:
        side = (dw + 1) // 2
        c0 = 0 if dw < 0 else 6
        @pl.when(jnp.logical_not(has[dl, dw]))
        def _():
            for h in range(2):
                for c in range(c0, c0 + 4):
                    for ref in (CT, KT, E0T):
                        ref[side, c, h, pl.ds(8 if dl < 0 else 48, 8), :] = jnp.zeros((8, 128), jnp.float32)

    for copy in loads:
        copy.wait()

    def prepare(i, carry):
        n = pl.multiple_of(32 * i, 32)
        o, p = pl.multiple_of(NAT0 + n, 32), pl.multiple_of(PAD + n, 8)
        for h in range(2):
            m = MAT[h, pl.ds(n, 32), :]
            b, g = B[h, pl.ds(n, 32), :], G[h, pl.ds(p, 32), :]
            hl = 0.5 * (U1[h, pl.ds(n, 32), :] * b)
            C[h, pl.ds(o, 32), :] = jnp.where(m == 0, 1.0, jnp.where(m == 1, 0.5, 6.0))
            K[h, pl.ds(o, 32), :] = WALL[h, pl.ds(n, 32), :].astype(jnp.float32)
            HL[h, pl.ds(n, 32), :] = hl
            HW[h, pl.ds(p, 32), :] = -0.5 * (U0[h, pl.ds(n, 32), :] * b)
            QP[h, pl.ds(o, 32), :] = g + hl
            QM[h, pl.ds(o, 32), :] = g - hl
        return carry

    lax.fori_loop(0, 32, prepare, 0)

    def column(ref, h, first, col, rows=32):
        return ref[h, pl.ds(first + col, rows, stride=32), :]

    own_t = pl.ds(TOWN, 32)
    for side in range(2):
        for col in range(0, 6) if side == 0 else range(26, 32):
            c = col - FIRST[side]
            for h in range(2):
                CT[side, c, h, own_t, :] = column(C, h, NAT0, col)
                KT[side, c, h, own_t, :] = column(K, h, NAT0, col)
                if 3 <= c <= 6:
                    GT[side, c, h, own_t, :] = column(G, h, PAD, col)
    for h in range(2):
        QS[0, h] = GT[0, 4, h, own_t, :] - column(HW, h, PAD, 0)
        QS[1, h] = GT[1, 5, h, own_t, :] + column(HW, h, PAD, 31)

    sent = []

    def message(way, src, dst):
        k = len(sent)
        copy = pltpu.make_async_remote_copy(
            src, dst, ssem.at[k], rsem.at[k], device_id=(li + way[0], wi + way[1]), device_id_type=MESH
        )
        sent.append((way, copy))
        @pl.when(has[way])
        def _():
            copy.start()
        return way, copy

    def received(messages):
        for way, copy in messages:
            @pl.when(has[-way[0], -way[1]])
            def _():
                copy.wait_recv()

    def nat_part(ref, way, depth, here):
        if way[0] < 0:
            first = NAT0 if here else NAT0 + 1024
        else:
            first = NAT0 + 1024 - 32 * depth if here else NAT0 - 32 * depth
        return ref.at[:, pl.ds(first, 32 * depth), :]

    def strip_part(ref, way, near, far, here):
        count = far - near + 1
        if way[1] < 0:
            side, first = (0, 3 + near) if here else (1, 5 + near)
        else:
            side, first = (1, 6 - far) if here else (0, 4 - far)
        if way[0] == 0:
            rows = own_t
        elif way[0] < 0:
            rows = pl.ds(16 if here else 48, 8)
        else:
            rows = pl.ds(40 if here else 8, 8)
        return ref.at[side, pl.ds(first, count), :, rows, :]

    pl.semaphore_wait(barrier, sum(has[way].astype(jnp.int32) for way in straight))

    wid_ways, len_ways = straight[:2], straight[2:]
    first_wid, first_len, later_len, later_wid = [], [], [], []
    for way in wid_ways:
        out, into = (0, 1) if way[1] < 0 else (1, 0)
        first_wid.append(message(way, QS.at[out], QR.at[into]))
        first_wid.append(message(way, strip_part(CT, way, 1, 1, True), strip_part(CT, way, 1, 1, False)))
    for way in len_ways:
        Q = QM if way[0] < 0 else QP
        first_len.append(message(way, nat_part(Q, way, 1, True), nat_part(Q, way, 1, False)))
        first_len.append(message(way, nat_part(C, way, 4, True), nat_part(C, way, 4, False)))
    for way in wid_ways:
        later_wid.append(message(way, strip_part(CT, way, 2, 4, True), strip_part(CT, way, 2, 4, False)))
        later_wid.append(message(way, strip_part(KT, way, 1, 3, True), strip_part(KT, way, 1, 3, False)))
        later_wid.append(message(way, strip_part(GT, way, 1, 1, True), strip_part(GT, way, 1, 1, False)))
    for way in len_ways:
        into = 1 if way[0] < 0 else 0
        first = PAD if way[0] < 0 else PAD + 31 * 32
        later_len.append(message(way, nat_part(K, way, 3, True), nat_part(K, way, 3, False)))
        later_len.append(message(way, G.at[:, pl.ds(first, 32), :], GH.at[into]))

    shape = (32, 128)
    jj = lax.broadcasted_iota(jnp.int32, shape, 0)
    lane = lanes_of(shape)

    def put_coefficients(iv, h, s, store):
        for q in range(6):
            t = s[q] * iv
            if q == 4 and h == 0:
                t = jnp.where(lanes_of(t.shape) == 0, 0.0, t)
            if q == 5 and h == 1:
                t = jnp.where(lanes_of(t.shape) == 127, 0.0, t)
            store(q, t)

    def row(i, valid=None):
        n = pl.multiple_of(32 * i, 32)
        o = pl.multiple_of(NAT0 + n, 32)
        p = pl.multiple_of(PAD + n, 8)
        c = [C[h, pl.ds(o, 32), :] for h in range(2)]
        cu, cd = k_up(c, True), k_down(c, True)
        if valid is None:
            g = [G[h, pl.ds(p, 32), :] for h in range(2)]
            gu, gd = k_up(g, True), k_down(g, True)
        for h in range(2):
            slm = 0.5 * (c[h] + C[h, pl.ds(o - 32, 32), :])
            slp = 0.5 * (c[h] + C[h, pl.ds(o + 32, 32), :])
            swm = jnp.where(jj == 0, 0.0, 0.5 * (c[h] + C[h, pl.ds(o - 1, 32), :]))
            swp = jnp.where(jj == 31, 0.0, 0.5 * (c[h] + C[h, pl.ds(o + 1, 32), :]))
            skm, skp = 0.5 * (c[h] + cd[h]), 0.5 * (c[h] + cu[h])
            k2 = 2.0 * K[h, pl.ds(o, 32), :]
            diag = k2 + ((slm + slp) + (swm + swp)) + (skm + skp)
            iv = 1.0 / diag
            if valid is None:
                hl, hw = HL[h, pl.ds(n, 32), :], HW[h, pl.ds(p, 32), :]
                gwm = jnp.where(jj == 0, 0.0, G[h, pl.ds(p - 1, 32), :] + HW[h, pl.ds(p - 1, 32), :] + hw)
                gwp = jnp.where(jj == 31, 0.0, G[h, pl.ds(p + 1, 32), :] - HW[h, pl.ds(p + 1, 32), :] - hw)
                res = slm * (QP[h, pl.ds(o - 32, 32), :] + hl) + slp * (QM[h, pl.ds(o + 32, 32), :] - hl)
                res = res + (swm * gwm + swp * gwp) + (skm * gd[h] + skp * gu[h]) - diag * g[h]
                RP[h, pl.ds(n, 32), :] = res
                DP[h, pl.ds(n, 32), :] = diag
                E0[h, pl.ds(o, 32), :] = res * iv
            else:
                iv = jnp.where(valid, iv, 0.0)

            def store(q, t):
                TN[q, h, pl.ds(o, 32), :] = t

            put_coefficients(iv, h, (slm, slp, swm, swp, skm, skp), store)

    def row_step(i, carry):
        row(i)
        return carry

    lax.fori_loop(1, 31, row_step, 0)

    received(first_len)
    row(0)
    row(31)
    later_diag = []
    for way in diagonal:
        later_diag.append(message(way, strip_part(CT, way, 1, 4, True), strip_part(CT, way, 1, 4, False)))
        later_diag.append(message(way, strip_part(KT, way, 1, 4, True), strip_part(KT, way, 1, 4, False)))

    received(first_wid)
    for side, col, halo, sign in ((0, 0, 3, 1.0), (1, 31, 6, -1.0)):
        for h in range(2):
            c = CT[side, col - FIRST[side], h, own_t, :]
            s = 0.5 * (c + CT[side, halo, h, own_t, :])
            res = column(RP, h, 0, col) + s * (
                QR[side, h] + sign * column(HW, h, PAD, col) - column(G, h, PAD, col)
            )
            e = res / (column(DP, h, 0, col) + s)
            E0T[side, col - FIRST[side], h, own_t, :] = e
            E0[h, pl.ds(NAT0 + col, 32, stride=32), :] = e
    for side in range(2):
        for col in range(1, 4) if side == 0 else range(28, 31):
            for h in range(2):
                E0T[side, col - FIRST[side], h, own_t, :] = column(E0, h, NAT0, col)

    second = []
    for way in wid_ways:
        second.append(message(way, strip_part(E0T, way, 1, 4, True), strip_part(E0T, way, 1, 4, False)))
    for way in diagonal:
        second.append(message(way, strip_part(E0T, way, 1, 4, True), strip_part(E0T, way, 1, 4, False)))
    for way in len_ways:
        second.append(message(way, nat_part(E0, way, 4, True), nat_part(E0, way, 4, False)))

    for side in range(2):
        for col in range(4, 6) if side == 0 else range(26, 28):
            for h in range(2):
                E0T[side, col - FIRST[side], h, own_t, :] = column(E0, h, NAT0, col)

    E = (E0, E1, E2, E3)
    ET = (E0T, E1T, E2T, E3T)

    def sweep_row(k, r):
        o = pl.multiple_of(32 * r, 32)
        src = E[k]
        x = [src[h, pl.ds(o, 32), :] for h in range(2)]
        xu, xd = k_up(x, False), k_down(x, False)
        for h in range(2):
            def t(q):
                return TN[q, h, pl.ds(o, 32), :]
            total = ALPHAS[k] * x[h] + t(4) * xd[h] + t(5) * xu[h]
            total = total + t(0) * src[h, pl.ds(o - 32, 32), :] + t(1) * src[h, pl.ds(o + 32, 32), :]
            total = total + t(2) * src[h, pl.ds(o - 1, 32), :] + t(3) * src[h, pl.ds(o + 1, 32), :]
            if k > 0:
                total = total + BETAS[k] * E[k - 1][h, pl.ds(o, 32), :]
            E[k + 1][h, pl.ds(o, 32), :] = total

    def sweep(k, first, last):
        def step(r, carry):
            sweep_row(k, r)
            return carry
        lax.fori_loop(first + DEEP, last + 1 + DEEP, step, 0)

    def potential_row(i, guess):
        o = pl.multiple_of(NAT0 + 32 * i, 32)
        q = pl.multiple_of(PW * (i + DEEP) + 8, 8)
        for h in range(2):
            total = guess(h)
            for k in range(SWEEPS):
                total = total + GAINS[k] * E[k][h, pl.ds(o, 32), :]
            POT[h, pl.ds(q, 32), :] = total

    def own_potential(first, last):
        def step(i, carry):
            p = pl.multiple_of(PAD + 32 * i, 8)
            potential_row(i, lambda h: G[h, pl.ds(p, 32), :])
            return carry
        lax.fori_loop(first, last + 1, step, 0)

    sweep(0, 1, 30)
    sweep(1, 2, 29)
    sweep(2, 3, 28)
    own_potential(3, 28)

    def force(i, carry):
        n = pl.multiple_of(32 * i, 32)
        o, p = pl.multiple_of(NAT0 + n, 32), pl.multiple_of(PAD + n, 8)
        for h in range(2):
            at = (h, pl.ds(n, 32), slice(None))
            cb = C[h, pl.ds(o, 32), :] * B[at]
            U0[at] = U0[at] + cb * HW[h, pl.ds(p, 32), :]
            U1[at] = U1[at] - cb * HL[at]
            B[at] = 0.25 * cb
        return carry

    lax.fori_loop(0, 32, force, 0)

    received(later_len)
    received(later_wid)
    received(later_diag)
    for i in (-3, -2, -1):
        row(i, has[-1, 0])
        row(31 - i, has[1, 0])
    for side in range(2):
        for col in range(0, 6) if side == 0 else range(26, 32):
            c = col - FIRST[side]
            for h in range(2):
                CT[side, c, h, pl.ds(12, 4), :] = column(C, h, 0, col, 4)
                CT[side, c, h, pl.ds(48, 4), :] = column(C, h, NAT0 + 1024, col, 4)
                KT[side, c, h, pl.ds(13, 3), :] = column(K, h, 32, col, 3)
                KT[side, c, h, pl.ds(48, 3), :] = column(K, h, NAT0 + 1024, col, 3)

    ii = lax.broadcasted_iota(jnp.int32, (40, 128), 0)
    rows_in = jnp.logical_and(
        jnp.logical_or(ii >= 4, has[-1, 0]), jnp.logical_or(ii < 36, has[1, 0])
    )

    for side in range(2):
        has_side = has[0, -1 if side == 0 else 1]

        def strip(c, carry):
            x = [CT[side, c, h, TAREA, :] for h in range(2)]
            cu, cd = k_up(x, True), k_down(x, True)
            in_own = c >= 4 if side == 0 else c < 6
            valid = jnp.logical_and(rows_in, jnp.logical_or(in_own, has_side))
            for h in range(2):
                slm = 0.5 * (x[h] + CT[side, c, h, pl.ds(11, 40), :])
                slp = 0.5 * (x[h] + CT[side, c, h, pl.ds(13, 40), :])
                swm = 0.5 * (x[h] + CT[side, c - 1, h, TAREA, :])
                swp = 0.5 * (x[h] + CT[side, c + 1, h, TAREA, :])
                skm, skp = 0.5 * (x[h] + cd[h]), 0.5 * (x[h] + cu[h])
                diag = 2.0 * KT[side, c, h, TAREA, :] + ((slm + slp) + (swm + swp)) + (skm + skp)
                iv = jnp.where(valid, 1.0 / diag, 0.0)

                def store(q, t):
                    TT[q, side, c, h, TAREA, :] = t

                put_coefficients(iv, h, (slm, slp, swm, swp, skm, skp), store)
            return carry

        lax.fori_loop(1, 9, strip, 0)

    received(second)

    for side in range(2):
        for col in range(0, 6) if side == 0 else range(26, 32):
            c = col - FIRST[side]
            for h in range(2):
                E0T[side, c, h, pl.ds(12, 4), :] = column(E0, h, 0, col, 4)
                E0T[side, c, h, pl.ds(48, 4), :] = column(E0, h, NAT0 + 1024, col, 4)

    for k in range(SWEEPS - 1):
        for side in range(2):
            def strip_sweep(c, carry):
                src = ET[k]
                x = [src[side, c, h, TAREA, :] for h in range(2)]
                xu, xd = k_up(x, False), k_down(x, False)
                for h in range(2):
                    def t(q):
                        return TT[q, side, c, h, TAREA, :]
                    total = ALPHAS[k] * x[h] + t(4) * xd[h] + t(5) * xu[h]
                    total = total + t(0) * src[side, c, h, pl.ds(11, 40), :] + t(1) * src[side, c, h, pl.ds(13, 40), :]
                    total = total + t(2) * src[side, c - 1, h, TAREA, :] + t(3) * src[side, c + 1, h, TAREA, :]
                    if k > 0:
                        total = total + BETAS[k] * ET[k - 1][side, c, h, TAREA, :]
                    ET[k + 1][side, c, h, TAREA, :] = total
                return carry

            lax.fori_loop(1 + k, 9 - k, strip_sweep, 0)
        sweep(k, k - 3, k)
        sweep(k, 31 - k, 34 - k)

    own_potential(0, 2)
    own_potential(29, 31)
    potential_row(-1, lambda h: GH[0, h])
    potential_row(32, lambda h: GH[1, h])
    for side in range(2):
        for c in range(3, 7):
            col = c + FIRST[side]
            for h in range(2):
                if 0 <= col < 32:
                    GT[side, c, h, pl.ds(15, 1), :] = GH[0, h, pl.ds(col, 1), :]
                    GT[side, c, h, pl.ds(48, 1), :] = GH[1, h, pl.ds(col, 1), :]
                total = GT[side, c, h, TAREA, :]
                for k in range(SWEEPS):
                    total = total + GAINS[k] * ET[k][side, c, h, TAREA, :]
                POT[h, pl.ds(8 + col, 40, stride=PW), :] = total

    def finish(i, carry):
        n = pl.multiple_of(32 * i, 32)
        q = pl.multiple_of(PW * (i + DEEP) + 8, 8)
        for h in range(2):
            at = (h, pl.ds(n, 32), slice(None))
            lanes = pl.ds(128 * h, 128)
            pot_out[pl.ds(n, 32), lanes] = POT[h, pl.ds(q, 32), :]
            vel_out[0, pl.ds(n, 32), lanes] = U0[at] - B[at] * (
                POT[h, pl.ds(q + 1, 32), :] - POT[h, pl.ds(q - 1, 32), :]
            )
            vel_out[1, pl.ds(n, 32), lanes] = U1[at] + B[at] * (
                POT[h, pl.ds(q + PW, 32), :] - POT[h, pl.ds(q - PW, 32), :]
            )
        return carry

    lax.fori_loop(0, 32, finish, 0)

    for way, copy in sent:
        @pl.when(has[way])
        def _():
            copy.wait_send()


N_MESSAGES = 34


def solution(mesh):
    n_len, n_wid = mesh.shape["len"], mesh.shape["wid"]

    def body(velocity, bfield, material, wall_mask, potential_guess):
        flat = lambda a: a.reshape(a.shape[:-3] + (1024, 256))
        own = pltpu.VMEM((2, 1024, 128), jnp.float32)
        padded = pltpu.VMEM((2, 1024 + 2 * PAD, 128), jnp.float32)
        nat = pltpu.VMEM((2, 1024 + 2 * NAT0, 128), jnp.float32)
        strip = pltpu.VMEM((2, 10, 2, TROWS, 128), jnp.float32)
        ints = pltpu.VMEM((2, 1024, 128), jnp.int32)
        rows = pltpu.VMEM((2, 2, 32, 128), jnp.float32)
        scratch = [
            own, own, own, ints, ints, padded, own, padded, nat, nat, nat, nat, own, own, nat, nat, nat, nat,
            pltpu.VMEM((6, 2, 1024 + 2 * NAT0, 128), jnp.float32), rows,
            strip, strip, strip, rows, rows, strip, strip, strip, strip,
            pltpu.VMEM((6, 2, 10, 2, TROWS, 128), jnp.float32),
            pltpu.VMEM((2, 40 * PW, 128), jnp.float32),
            pltpu.SemaphoreType.DMA((12,)),
            pltpu.SemaphoreType.DMA((N_MESSAGES,)),
            pltpu.SemaphoreType.DMA((N_MESSAGES,)),
        ]
        vel, pot = pl.pallas_call(
            functools.partial(kernel, n_len, n_wid),
            out_shape=(
                jax.ShapeDtypeStruct((2, 1024, 256), jnp.float32),
                jax.ShapeDtypeStruct((1024, 256), jnp.float32),
            ),
            in_specs=[pl.BlockSpec(memory_space=pltpu.HBM)] * 5,
            out_specs=(pl.BlockSpec(memory_space=pltpu.VMEM), pl.BlockSpec(memory_space=pltpu.VMEM)),
            scratch_shapes=scratch,
            compiler_params=pltpu.CompilerParams(
                collective_id=0, has_side_effects=True, vmem_limit_bytes=58 * 1024 * 1024
            ),
        )(flat(velocity), flat(bfield), flat(material), flat(wall_mask), flat(potential_guess))
        return vel.reshape(velocity.shape), pot.reshape(bfield.shape)

    whole, part = P(None, "len", "wid", None), P("len", "wid", None)
    return jax.shard_map(
        body,
        mesh=mesh,
        in_specs=(whole, part, part, part, part),
        out_specs=(whole, part),
        check_vma=False,
    )
```

time: 129 us -> 39.4 us (0.31); the launches traced: 127 us -> 39.2 us
  starting transfers between devices: 60 us -> 0 us
  Pallas kernels: 0 us -> 34.4 us
  waiting for transfers between devices: 33.2 us -> 0 us
  other arithmetic: 25.1 us -> 0 us
  local copies, waits for them, and re-layouts: 7.23 us -> 4.22 us
    ppermute x20 -> x0, starting transfers between devices: 60 us -> none  [the longest x10 32.4 us: padded(): lax.ppermute(tail, axis, [(i, (i + 1) % count) for i in range(ends)])]
    pallas_call x0 -> x1, Pallas kernels: none -> 34.4 us  [body(): pl.pallas_call(functools.partial(kernel, n_len, n_wid), out_shape=(jax.Sh...]
    ppermute x20 -> x0, waiting for transfers between devices: 33.2 us -> none  [the longest x10 17.3 us: padded(): lax.ppermute(tail, axis, [(i, (i + 1) % count) for i in range(ends)])]
    mul x4 -> x0, other arithmetic: 11.5 us -> none  [the longest x2 6.07 us: body(): direction = direction * inside_mask(rows_dev, cols_dev, margin_dir - 1)]
    slice x9 -> x0, local copies, waits for them, and re-layouts: 4.31 us -> none  [the longest x1 2.43 us: downward(): field[:, :, :-1]]
    unnamed x4 -> x0, other arithmetic: 3.81 us -> none
    add x1 -> x0, other arithmetic: 3.34 us -> none  [body(): potential = potential + trim_margin(direction, margin_dir, 0)]
    another operation x2 -> x0, other arithmetic: 2.88 us -> none  [body(): return (jnp.stack([new_len, new_wid]), potential)]
  transfers between devices with their start and end apart: 20 -> 0, of which waited for: 12 -> 0; matrix products, arithmetic and copies ran while one was open for 1% -> 0% of each run, Pallas kernels for 0% -> 0%
where the time goes in v1:
time: 39.4 us; the launch traced here: 39.2 us
  Pallas kernels  34.4 us (87%)
  local copies, waits for them, and re-layouts  4.22 us (11%)
  between operations  0.65 us (2%)
    pallas_call x1, Pallas kernels, body(): pl.pallas_call(functools.partial(kernel, n_len, n_wid), out_shape=(jax.Sh...  34.4 us
    unnamed x4, local copies, waits for them, and re-layouts  4.22 us

profile of v1, /device:TPU:27, one launch (start us, length us, event | category | flops | bytes accessed | tf_op | source)
XLA Modules:
  0.0 39.2 jit_solution(8211117628966973441)
XLA Ops:
  0.6 34.4 %shard_map.68 = (f32[2,1024,256]{2,1,0:T(8,128)}, f32[1024,256]{1,0:T(8,128)}) custom-call(f32[2,1024,256]{2,1,0:T(8,128)} %bitcast.7, f32[1024,256]{1,0:T(8,128)} %bitcast.10, s32[1024,256]{1,0:T(8,128)} %bitcast.11, s32[1024,256]{1,0:T(8,128)} %bitcast.12, f32[1024,256]{1,0:T(8,128)} %bitcast.13), custom_call_target="tpu_custom_call" | custom-call | tf_op jit(solution)/shard_map/pallas_call | solution.py:506
  35.0 0.0 copy-start
  35.0 3.2 %copy.9 = f32[2,32,32,256]{3,2,1,0:T(8,128)} copy(f32[2,32,32,256]{3,2,1,0:T(8,128)} %bitcast.8) | data formatting | bytes 4194304
  38.3 0.0 copy-done
  38.3 1.0 %copy.10 = f32[32,32,256]{2,1,0:T(8,128)} copy(f32[32,32,256]{2,1,0:T(8,128)S(1)} %bitcast.9) | data formatting | bytes 2097152
Async XLA Ops:
  35.0 3.3 %copy-start = (f32[1024,256]{1,0:T(8,128)S(1)}, f32[1024,256]{1,0:T(8,128)}, u32[]{:S(2)}) copy-start(f32[1024,256]{1,0:T(8,128)} %get-tuple-element.5) | copy-start | bytes 3145732

commit v2 on v1

--- a/solution.py
+++ b/solution.py
@@ -136,7 +136,7 @@
             QM[h, pl.ds(o, 32), :] = g - hl
         return carry
 
-    lax.fori_loop(0, 32, prepare, 0)
+    lax.fori_loop(0, 32, prepare, 0, unroll=2)
 
     def column(ref, h, first, col, rows=32):
         return ref[h, pl.ds(first + col, rows, stride=32), :]
@@ -189,9 +189,9 @@
         if way[0] == 0:
             rows = own_t
         elif way[0] < 0:
-            rows = pl.ds(16 if here else 48, 8)
+            rows = pl.ds(16 if here else 48, 4)
         else:
-            rows = pl.ds(40 if here else 8, 8)
+            rows = pl.ds(44 if here else 12, 4)
         return ref.at[side, pl.ds(first, count), :, rows, :]
 
     pl.semaphore_wait(barrier, sum(has[way].astype(jnp.int32) for way in straight))
@@ -268,15 +268,15 @@
         row(i)
         return carry
 
-    lax.fori_loop(1, 31, row_step, 0)
+    lax.fori_loop(1, 31, row_step, 0, unroll=2)
 
     received(first_len)
     row(0)
     row(31)
     later_diag = []
     for way in diagonal:
-        later_diag.append(message(way, strip_part(CT, way, 1, 4, True), strip_part(CT, way, 1, 4, False)))
-        later_diag.append(message(way, strip_part(KT, way, 1, 4, True), strip_part(KT, way, 1, 4, False)))
+        later_diag.append(message(way, strip_part(CT, way, 1, 3, True), strip_part(CT, way, 1, 3, False)))
+        later_diag.append(message(way, strip_part(KT, way, 1, 2, True), strip_part(KT, way, 1, 2, False)))
 
     received(first_wid)
     for side, col, halo, sign in ((0, 0, 3, 1.0), (1, 31, 6, -1.0)):
@@ -298,7 +298,7 @@
     for way in wid_ways:
         second.append(message(way, strip_part(E0T, way, 1, 4, True), strip_part(E0T, way, 1, 4, False)))
     for way in diagonal:
-        second.append(message(way, strip_part(E0T, way, 1, 4, True), strip_part(E0T, way, 1, 4, False)))
+        second.append(message(way, strip_part(E0T, way, 1, 3, True), strip_part(E0T, way, 1, 3, False)))
     for way in len_ways:
         second.append(message(way, nat_part(E0, way, 4, True), nat_part(E0, way, 4, False)))
 
@@ -329,7 +329,7 @@
         def step(r, carry):
             sweep_row(k, r)
             return carry
-        lax.fori_loop(first + DEEP, last + 1 + DEEP, step, 0)
+        lax.fori_loop(first + DEEP, last + 1 + DEEP, step, 0, unroll=4)
 
     def potential_row(i, guess):
         o = pl.multiple_of(NAT0 + 32 * i, 32)
@@ -345,7 +345,7 @@
             p = pl.multiple_of(PAD + 32 * i, 8)
             potential_row(i, lambda h: G[h, pl.ds(p, 32), :])
             return carry
-        lax.fori_loop(first, last + 1, step, 0)
+        lax.fori_loop(first, last + 1, step, 0, unroll=2)
 
     sweep(0, 1, 30)
     sweep(1, 2, 29)
@@ -408,7 +408,8 @@
                 put_coefficients(iv, h, (slm, slp, swm, swp, skm, skp), store)
             return carry
 
-        lax.fori_loop(1, 9, strip, 0)
+        for c in range(1, 9):
+            strip(c, 0)
 
     received(second)
 
@@ -436,7 +437,8 @@
                     ET[k + 1][side, c, h, TAREA, :] = total
                 return carry
 
-            lax.fori_loop(1 + k, 9 - k, strip_sweep, 0)
+            for c in range(1 + k, 9 - k):
+                strip_sweep(c, 0)
         sweep(k, k - 3, k)
         sweep(k, 31 - k, 34 - k)
 
@@ -471,7 +473,7 @@
             )
         return carry
 
-    lax.fori_loop(0, 32, finish, 0)
+    lax.fori_loop(0, 32, finish, 0, unroll=2)
 
     for way, copy in sent:
         @pl.when(has[way])
@@ -486,7 +488,7 @@
     n_len, n_wid = mesh.shape["len"], mesh.shape["wid"]
 
     def body(velocity, bfield, material, wall_mask, potential_guess):
-        flat = lambda a: a.reshape(a.shape[:-3] + (1024, 256))
+        flat = lambda a: pltpu.with_memory_space_constraint(a.reshape(a.shape[:-3] + (1024, 256)), pltpu.HBM)
         own = pltpu.VMEM((2, 1024, 128), jnp.float32)
         padded = pltpu.VMEM((2, 1024 + 2 * PAD, 128), jnp.float32)
         nat = pltpu.VMEM((2, 1024 + 2 * NAT0, 128), jnp.float32)
@@ -506,14 +508,14 @@
         vel, pot = pl.pallas_call(
             functools.partial(kernel, n_len, n_wid),
             out_shape=(
-                jax.ShapeDtypeStruct((2, 1024, 256), jnp.float32),
-                jax.ShapeDtypeStruct((1024, 256), jnp.float32),
+                pltpu.VMEM((2, 1024, 256), jnp.float32),
+                pltpu.VMEM((1024, 256), jnp.float32),
             ),
             in_specs=[pl.BlockSpec(memory_space=pltpu.HBM)] * 5,
             out_specs=(pl.BlockSpec(memory_space=pltpu.VMEM), pl.BlockSpec(memory_space=pltpu.VMEM)),
             scratch_shapes=scratch,
             compiler_params=pltpu.CompilerParams(
-                collective_id=0, has_side_effects=True, vmem_limit_bytes=58 * 1024 * 1024
+                collective_id=0, has_side_effects=True, vmem_limit_bytes=50 * 1024 * 1024
             ),
         )(flat(velocity), flat(bfield), flat(material), flat(wall_mask), flat(potential_guess))
         return vel.reshape(velocity.shape), pot.reshape(bfield.shape)

time: 39.4 us -> 28.5 us (0.72)
  Pallas kernels: 34.4 us -> 25.5 us
  local copies, waits for them, and re-layouts: 4.22 us -> 2.29 us
    pallas_call x1, Pallas kernels: 34.4 us -> 25.5 us  [body(): pl.pallas_call(functools.partial(kernel, n_len, n_wid), out_shape=(pltpu....]
    unnamed x4 -> x2, local copies, waits for them, and re-layouts: 4.22 us -> 2.29 us
where the time goes in v2:
time: 28.5 us
  Pallas kernels  25.5 us (89%)
  local copies, waits for them, and re-layouts  2.29 us (8%)
  between operations  0.64 us (2%)
    pallas_call x1, Pallas kernels, body(): pl.pallas_call(functools.partial(kernel, n_len, n_wid), out_shape=(pltpu....  25.5 us
    unnamed x2, local copies, waits for them, and re-layouts  2.29 us

profile of v2, /device:TPU:27, one launch (start us, length us, event | category | flops | bytes accessed | tf_op | source)
XLA Modules:
  0.0 28.5 jit_solution(7747078452853193408)
XLA Ops:
  0.6 25.5 %shard_map.68 = (f32[2,1024,256]{2,1,0:T(8,128)S(1)}, f32[1024,256]{1,0:T(8,128)S(1)}) custom-call(f32[2,1024,256]{2,1,0:T(8,128)} %bitcast.9, f32[1024,256]{1,0:T(8,128)} %bitcast.10, s32[1024,256]{1,0:T(8,128)} %bitcast.11, s32[1024,256]{1,0:T(8,128)} %bitcast.12, f32[1024,256]{1,0:T(8,128)} %bitcast.13), custom_call_target="tpu_custom_call" | custom-call | tf_op jit(solution)/shard_map/pallas_call | solution.py:508
  26.2 1.3 %copy.9 = f32[2,32,32,256]{3,2,1,0:T(8,128)} copy(f32[2,32,32,256]{3,2,1,0:T(8,128)S(1)} %bitcast.7) | data formatting | bytes 4194304
  27.5 1.0 %copy.10 = f32[32,32,256]{2,1,0:T(8,128)} copy(f32[32,32,256]{2,1,0:T(8,128)S(1)} %bitcast.8) | data formatting | bytes 2097152

commit v3 on v2

--- a/solution.py
+++ b/solution.py
@@ -22,6 +22,7 @@
 TAREA = pl.ds(12, 40)
 PW = 48
 FIRST = (-4, 26)
+OWN_COLS = (range(0, 4), range(28, 32))
 
 
 def chebyshev():
@@ -62,7 +63,7 @@
 
 
 def kernel(n_len, n_wid, u_hbm, b_hbm, m_hbm, w_hbm, g_hbm, vel_out, pot_out,
-           U0, U1, B, MAT, WALL, G, HL, HW, QP, QM, C, K, RP, DP, E0, E1, E2, E3, TN, GH,
+           U0, U1, B, MAT, WALL, G, HL, HW, QP, QM, C, K, RP, DP, E0, E1, E2, TN, GH,
            CT, KT, GT, QS, QR, E0T, E1T, E2T, E3T, TT, POT, lsem, ssem, rsem):
     li, wi = lax.axis_index("len"), lax.axis_index("wid")
     has = {(-1, 0): li > 0, (1, 0): li < n_len - 1, (0, -1): wi > 0, (0, 1): wi < n_wid - 1}
@@ -81,8 +82,8 @@
     own = pl.ds(PAD, 1024)
     loads = []
     for src, dst in (
-        (m_hbm, lambda h: MAT.at[h]), (g_hbm, lambda h: G.at[h, own]), (b_hbm, lambda h: B.at[h]),
-        (u_hbm.at[0], lambda h: U0.at[h]), (u_hbm.at[1], lambda h: U1.at[h]), (w_hbm, lambda h: WALL.at[h]),
+        (m_hbm, lambda h: MAT.at[h]), (u_hbm.at[0], lambda h: U0.at[h]), (b_hbm, lambda h: B.at[h]),
+        (g_hbm, lambda h: G.at[h, own]), (u_hbm.at[1], lambda h: U1.at[h]), (w_hbm, lambda h: WALL.at[h]),
     ):
         for h in range(2):
             copy = pltpu.make_async_copy(src.at[:, pl.ds(128 * h, 128)], dst(h), lsem.at[len(loads)])
@@ -118,7 +119,23 @@
                     for ref in (CT, KT, E0T):
                         ref[side, c, h, pl.ds(8 if dl < 0 else 48, 8), :] = jnp.zeros((8, 128), jnp.float32)
 
-    for copy in loads:
+    def column(ref, h, first, col, rows=32):
+        return ref[h, pl.ds(first + col, rows, stride=32), :]
+
+    def conduct(m):
+        return jnp.where(m == 0, 1.0, jnp.where(m == 1, 0.5, 6.0))
+
+    own_t = pl.ds(TOWN, 32)
+    edges = ((0, 0, 4, -1.0), (1, 31, 5, 1.0))
+    for copy in loads[:8]:
+        copy.wait()
+    for side, col, c, sign in edges:
+        for h in range(2):
+            g = column(G, h, PAD, col)
+            CT[side, c, h, own_t, :] = conduct(column(MAT, h, 0, col))
+            GT[side, c, h, own_t, :] = g
+            QS[side, h] = g - sign * (0.5 * (column(U0, h, 0, col) * column(B, h, 0, col)))
+    for copy in loads[8:]:
         copy.wait()
 
     def prepare(i, carry):
@@ -128,7 +145,7 @@
             m = MAT[h, pl.ds(n, 32), :]
             b, g = B[h, pl.ds(n, 32), :], G[h, pl.ds(p, 32), :]
             hl = 0.5 * (U1[h, pl.ds(n, 32), :] * b)
-            C[h, pl.ds(o, 32), :] = jnp.where(m == 0, 1.0, jnp.where(m == 1, 0.5, 6.0))
+            C[h, pl.ds(o, 32), :] = conduct(m)
             K[h, pl.ds(o, 32), :] = WALL[h, pl.ds(n, 32), :].astype(jnp.float32)
             HL[h, pl.ds(n, 32), :] = hl
             HW[h, pl.ds(p, 32), :] = -0.5 * (U0[h, pl.ds(n, 32), :] * b)
@@ -136,23 +153,7 @@
             QM[h, pl.ds(o, 32), :] = g - hl
         return carry
 
-    lax.fori_loop(0, 32, prepare, 0, unroll=2)
-
-    def column(ref, h, first, col, rows=32):
-        return ref[h, pl.ds(first + col, rows, stride=32), :]
-
-    own_t = pl.ds(TOWN, 32)
-    for side in range(2):
-        for col in range(0, 6) if side == 0 else range(26, 32):
-            c = col - FIRST[side]
-            for h in range(2):
-                CT[side, c, h, own_t, :] = column(C, h, NAT0, col)
-                KT[side, c, h, own_t, :] = column(K, h, NAT0, col)
-                if 3 <= c <= 6:
-                    GT[side, c, h, own_t, :] = column(G, h, PAD, col)
-    for h in range(2):
-        QS[0, h] = GT[0, 4, h, own_t, :] - column(HW, h, PAD, 0)
-        QS[1, h] = GT[1, 5, h, own_t, :] + column(HW, h, PAD, 31)
+    lax.fori_loop(0, 32, prepare, 0, unroll=4)
 
     sent = []
 
@@ -206,6 +207,15 @@
         Q = QM if way[0] < 0 else QP
         first_len.append(message(way, nat_part(Q, way, 1, True), nat_part(Q, way, 1, False)))
         first_len.append(message(way, nat_part(C, way, 4, True), nat_part(C, way, 4, False)))
+    for side in range(2):
+        for col in OWN_COLS[side]:
+            c = col - FIRST[side]
+            for h in range(2):
+                if col not in (0, 31):
+                    CT[side, c, h, own_t, :] = column(C, h, NAT0, col)
+                    if 3 <= c <= 6:
+                        GT[side, c, h, own_t, :] = column(G, h, PAD, col)
+                KT[side, c, h, own_t, :] = column(K, h, NAT0, col)
     for way in wid_ways:
         later_wid.append(message(way, strip_part(CT, way, 2, 4, True), strip_part(CT, way, 2, 4, False)))
         later_wid.append(message(way, strip_part(KT, way, 1, 3, True), strip_part(KT, way, 1, 3, False)))
@@ -253,6 +263,11 @@
                 gwp = jnp.where(jj == 31, 0.0, G[h, pl.ds(p + 1, 32), :] - HW[h, pl.ds(p + 1, 32), :] - hw)
                 res = slm * (QP[h, pl.ds(o - 32, 32), :] + hl) + slp * (QM[h, pl.ds(o + 32, 32), :] - hl)
                 res = res + (swm * gwm + swp * gwp) + (skm * gd[h] + skp * gu[h]) - diag * g[h]
+                at = (h, pl.ds(n, 32), slice(None))
+                cb = c[h] * B[at]
+                U0[at] = U0[at] + cb * hw
+                U1[at] = U1[at] - cb * hl
+                B[at] = 0.25 * cb
                 RP[h, pl.ds(n, 32), :] = res
                 DP[h, pl.ds(n, 32), :] = diag
                 E0[h, pl.ds(o, 32), :] = res * iv
@@ -268,7 +283,7 @@
         row(i)
         return carry
 
-    lax.fori_loop(1, 31, row_step, 0, unroll=2)
+    lax.fori_loop(1, 31, row_step, 0, unroll=5)
 
     received(first_len)
     row(0)
@@ -278,39 +293,37 @@
         later_diag.append(message(way, strip_part(CT, way, 1, 3, True), strip_part(CT, way, 1, 3, False)))
         later_diag.append(message(way, strip_part(KT, way, 1, 2, True), strip_part(KT, way, 1, 2, False)))
 
+    for side in range(2):
+        for col in OWN_COLS[side]:
+            if col not in (0, 31):
+                for h in range(2):
+                    E0T[side, col - FIRST[side], h, own_t, :] = column(E0, h, NAT0, col)
+    second, second_len = [], []
+    for way in wid_ways:
+        second.append(message(way, strip_part(E0T, way, 2, 4, True), strip_part(E0T, way, 2, 4, False)))
+
     received(first_wid)
-    for side, col, halo, sign in ((0, 0, 3, 1.0), (1, 31, 6, -1.0)):
+    for side, col, c, sign in edges:
+        halo = c - 1 if side == 0 else c + 1
         for h in range(2):
-            c = CT[side, col - FIRST[side], h, own_t, :]
-            s = 0.5 * (c + CT[side, halo, h, own_t, :])
+            s = 0.5 * (CT[side, c, h, own_t, :] + CT[side, halo, h, own_t, :])
             res = column(RP, h, 0, col) + s * (
-                QR[side, h] + sign * column(HW, h, PAD, col) - column(G, h, PAD, col)
+                QR[side, h] - sign * column(HW, h, PAD, col) - GT[side, c, h, own_t, :]
             )
             e = res / (column(DP, h, 0, col) + s)
-            E0T[side, col - FIRST[side], h, own_t, :] = e
+            E0T[side, c, h, own_t, :] = e
             E0[h, pl.ds(NAT0 + col, 32, stride=32), :] = e
-    for side in range(2):
-        for col in range(1, 4) if side == 0 else range(28, 31):
-            for h in range(2):
-                E0T[side, col - FIRST[side], h, own_t, :] = column(E0, h, NAT0, col)
-
-    second = []
     for way in wid_ways:
-        second.append(message(way, strip_part(E0T, way, 1, 4, True), strip_part(E0T, way, 1, 4, False)))
+        second.append(message(way, strip_part(E0T, way, 1, 1, True), strip_part(E0T, way, 1, 1, False)))
     for way in diagonal:
         second.append(message(way, strip_part(E0T, way, 1, 3, True), strip_part(E0T, way, 1, 3, False)))
     for way in len_ways:
-        second.append(message(way, nat_part(E0, way, 4, True), nat_part(E0, way, 4, False)))
-
-    for side in range(2):
-        for col in range(4, 6) if side == 0 else range(26, 28):
-            for h in range(2):
-                E0T[side, col - FIRST[side], h, own_t, :] = column(E0, h, NAT0, col)
-
-    E = (E0, E1, E2, E3)
+        second_len.append(message(way, nat_part(E0, way, 4, True), nat_part(E0, way, 4, False)))
+
+    E = (E0, E1, E2)
     ET = (E0T, E1T, E2T, E3T)
 
-    def sweep_row(k, r):
+    def sweep_row(k, r, guess=None):
         o = pl.multiple_of(32 * r, 32)
         src = E[k]
         x = [src[h, pl.ds(o, 32), :] for h in range(2)]
@@ -322,63 +335,83 @@
             total = total + t(0) * src[h, pl.ds(o - 32, 32), :] + t(1) * src[h, pl.ds(o + 32, 32), :]
             total = total + t(2) * src[h, pl.ds(o - 1, 32), :] + t(3) * src[h, pl.ds(o + 1, 32), :]
             if k > 0:
-                total = total + BETAS[k] * E[k - 1][h, pl.ds(o, 32), :]
-            E[k + 1][h, pl.ds(o, 32), :] = total
-
-    def sweep(k, first, last):
+                old = E[k - 1][h, pl.ds(o, 32), :]
+                total = total + BETAS[k] * old
+            if k < SWEEPS - 2:
+                E[k + 1][h, pl.ds(o, 32), :] = total
+            else:
+                g = guess(h) if guess else G[h, pl.ds(pl.multiple_of(o - (NAT0 - PAD), 8), 32), :]
+                pot = (g + GAINS[0] * E0[h, pl.ds(o, 32), :]) + GAINS[1] * old
+                pot = (pot + GAINS[2] * x[h]) + GAINS[3] * total
+                POT[h, pl.ds(pl.multiple_of(PW * r + 8, 8), 32), :] = pot
+
+    def sweep(k, first, last, unroll):
         def step(r, carry):
             sweep_row(k, r)
             return carry
-        lax.fori_loop(first + DEEP, last + 1 + DEEP, step, 0, unroll=4)
-
-    def potential_row(i, guess):
-        o = pl.multiple_of(NAT0 + 32 * i, 32)
-        q = pl.multiple_of(PW * (i + DEEP) + 8, 8)
-        for h in range(2):
-            total = guess(h)
-            for k in range(SWEEPS):
-                total = total + GAINS[k] * E[k][h, pl.ds(o, 32), :]
-            POT[h, pl.ds(q, 32), :] = total
-
-    def own_potential(first, last):
-        def step(i, carry):
-            p = pl.multiple_of(PAD + 32 * i, 8)
-            potential_row(i, lambda h: G[h, pl.ds(p, 32), :])
-            return carry
-        lax.fori_loop(first, last + 1, step, 0, unroll=2)
-
-    sweep(0, 1, 30)
-    sweep(1, 2, 29)
-    sweep(2, 3, 28)
-    own_potential(3, 28)
-
-    def force(i, carry):
-        n = pl.multiple_of(32 * i, 32)
-        o, p = pl.multiple_of(NAT0 + n, 32), pl.multiple_of(PAD + n, 8)
-        for h in range(2):
-            at = (h, pl.ds(n, 32), slice(None))
-            cb = C[h, pl.ds(o, 32), :] * B[at]
-            U0[at] = U0[at] + cb * HW[h, pl.ds(p, 32), :]
-            U1[at] = U1[at] - cb * HL[at]
-            B[at] = 0.25 * cb
-        return carry
-
-    lax.fori_loop(0, 32, force, 0)
+        lax.fori_loop(first + DEEP, last + 1 + DEEP, step, 0, unroll=unroll)
+
+    sweep(0, 1, 30, 10)
+    sweep(1, 2, 29, 14)
+    sweep(2, 3, 28, 13)
 
     received(later_len)
     received(later_wid)
-    received(later_diag)
     for i in (-3, -2, -1):
         row(i, has[-1, 0])
         row(31 - i, has[1, 0])
     for side in range(2):
-        for col in range(0, 6) if side == 0 else range(26, 32):
+        for col in OWN_COLS[side]:
             c = col - FIRST[side]
             for h in range(2):
                 CT[side, c, h, pl.ds(12, 4), :] = column(C, h, 0, col, 4)
                 CT[side, c, h, pl.ds(48, 4), :] = column(C, h, NAT0 + 1024, col, 4)
-                KT[side, c, h, pl.ds(13, 3), :] = column(K, h, 32, col, 3)
-                KT[side, c, h, pl.ds(48, 3), :] = column(K, h, NAT0 + 1024, col, 3)
+                if 3 <= c <= 6:
+                    KT[side, c, h, pl.ds(13, 3), :] = column(K, h, 32, col, 3)
+                    KT[side, c, h, pl.ds(48, 3), :] = column(K, h, NAT0 + 1024, col, 3)
+                    GT[side, c, h, pl.ds(15, 1), :] = GH[0, h, pl.ds(col, 1), :]
+                    GT[side, c, h, pl.ds(48, 1), :] = GH[1, h, pl.ds(col, 1), :]
+
+    received(second_len)
+    for k in range(SWEEPS - 1):
+        for i in (*range(k - 3, k + 1), *range(31 - k, 35 - k)):
+            guess = None
+            if i == -1:
+                guess = lambda h: GH[0, h]
+            if i == 32:
+                guess = lambda h: GH[1, h]
+            sweep_row(k, i + DEEP, guess)
+    for side in range(2):
+        for col in OWN_COLS[side]:
+            c = col - FIRST[side]
+            for h in range(2):
+                E0T[side, c, h, pl.ds(12, 4), :] = column(E0, h, 0, col, 4)
+                E0T[side, c, h, pl.ds(48, 4), :] = column(E0, h, NAT0 + 1024, col, 4)
+                if col in (1, 2, 29, 30):
+                    E1T[side, c, h, TAREA, :] = column(E1, h, 0, col, 40)
+                if col in (2, 3, 28, 29):
+                    E2T[side, c, h, TAREA, :] = column(E2, h, 0, col, 40)
+
+    def finish(first, count, unroll):
+        def step(i, carry):
+            n = pl.multiple_of(32 * i + first, 8)
+            q = pl.multiple_of(PW * (i + DEEP) + 8 + first, 8)
+            for h in range(2):
+                at = (h, pl.ds(n, count), slice(None))
+                lanes = pl.ds(128 * h, 128)
+                pot_out[pl.ds(n, count), lanes] = POT[h, pl.ds(q, count), :]
+                vel_out[0, pl.ds(n, count), lanes] = U0[at] - B[at] * (
+                    POT[h, pl.ds(q + 1, count), :] - POT[h, pl.ds(q - 1, count), :]
+                )
+                vel_out[1, pl.ds(n, count), lanes] = U1[at] + B[at] * (
+                    POT[h, pl.ds(q + PW, count), :] - POT[h, pl.ds(q - PW, count), :]
+                )
+            return carry
+
+        lax.fori_loop(0, 32, step, 0, unroll=unroll)
+
+    finish(8, 16, 4)
+    received(later_diag)
 
     ii = lax.broadcasted_iota(jnp.int32, (40, 128), 0)
     rows_in = jnp.logical_and(
@@ -408,17 +441,10 @@
                 put_coefficients(iv, h, (slm, slp, swm, swp, skm, skp), store)
             return carry
 
-        for c in range(1, 9):
+        for c in range(1, 7) if side == 0 else range(3, 9):
             strip(c, 0)
 
     received(second)
-
-    for side in range(2):
-        for col in range(0, 6) if side == 0 else range(26, 32):
-            c = col - FIRST[side]
-            for h in range(2):
-                E0T[side, c, h, pl.ds(12, 4), :] = column(E0, h, 0, col, 4)
-                E0T[side, c, h, pl.ds(48, 4), :] = column(E0, h, NAT0 + 1024, col, 4)
 
     for k in range(SWEEPS - 1):
         for side in range(2):
@@ -437,43 +463,18 @@
                     ET[k + 1][side, c, h, TAREA, :] = total
                 return carry
 
-            for c in range(1 + k, 9 - k):
+            for c in range(1 + k, 5 + k) if side == 0 else range(5 - k, 9 - k):
                 strip_sweep(c, 0)
-        sweep(k, k - 3, k)
-        sweep(k, 31 - k, 34 - k)
-
-    own_potential(0, 2)
-    own_potential(29, 31)
-    potential_row(-1, lambda h: GH[0, h])
-    potential_row(32, lambda h: GH[1, h])
+
     for side in range(2):
         for c in range(3, 7):
-            col = c + FIRST[side]
-            for h in range(2):
-                if 0 <= col < 32:
-                    GT[side, c, h, pl.ds(15, 1), :] = GH[0, h, pl.ds(col, 1), :]
-                    GT[side, c, h, pl.ds(48, 1), :] = GH[1, h, pl.ds(col, 1), :]
+            for h in range(2):
                 total = GT[side, c, h, TAREA, :]
                 for k in range(SWEEPS):
                     total = total + GAINS[k] * ET[k][side, c, h, TAREA, :]
-                POT[h, pl.ds(8 + col, 40, stride=PW), :] = total
-
-    def finish(i, carry):
-        n = pl.multiple_of(32 * i, 32)
-        q = pl.multiple_of(PW * (i + DEEP) + 8, 8)
-        for h in range(2):
-            at = (h, pl.ds(n, 32), slice(None))
-            lanes = pl.ds(128 * h, 128)
-            pot_out[pl.ds(n, 32), lanes] = POT[h, pl.ds(q, 32), :]
-            vel_out[0, pl.ds(n, 32), lanes] = U0[at] - B[at] * (
-                POT[h, pl.ds(q + 1, 32), :] - POT[h, pl.ds(q - 1, 32), :]
-            )
-            vel_out[1, pl.ds(n, 32), lanes] = U1[at] + B[at] * (
-                POT[h, pl.ds(q + PW, 32), :] - POT[h, pl.ds(q - PW, 32), :]
-            )
-        return carry
-
-    lax.fori_loop(0, 32, finish, 0, unroll=2)
+                POT[h, pl.ds(8 + c + FIRST[side], 40, stride=PW), :] = total
+    finish(0, 8, 4)
+    finish(24, 8, 4)
 
     for way, copy in sent:
         @pl.when(has[way])
@@ -481,7 +482,7 @@
             copy.wait_send()
 
 
-N_MESSAGES = 34
+N_MESSAGES = 36
 
 
 def solution(mesh):
@@ -496,7 +497,7 @@
         ints = pltpu.VMEM((2, 1024, 128), jnp.int32)
         rows = pltpu.VMEM((2, 2, 32, 128), jnp.float32)
         scratch = [
-            own, own, own, ints, ints, padded, own, padded, nat, nat, nat, nat, own, own, nat, nat, nat, nat,
+            own, own, own, ints, ints, padded, own, padded, nat, nat, nat, nat, own, own, nat, nat, nat,
             pltpu.VMEM((6, 2, 1024 + 2 * NAT0, 128), jnp.float32), rows,
             strip, strip, strip, rows, rows, strip, strip, strip, strip,
             pltpu.VMEM((6, 2, 10, 2, TROWS, 128), jnp.float32),

time: 28.5 us -> 26.7 us (0.937)
  Pallas kernels: 25.5 us -> 23.7 us
    pallas_call x1, Pallas kernels: 25.5 us -> 23.7 us  [body(): pl.pallas_call(functools.partial(kernel, n_len, n_wid), out_shape=(pltpu....]
where the time goes in v3:
time: 26.7 us; the launch traced here: 26.6 us
  Pallas kernels  23.7 us (89%)
  local copies, waits for them, and re-layouts  2.29 us (9%)
  between operations  0.64 us (2%)
    pallas_call x1, Pallas kernels, body(): pl.pallas_call(functools.partial(kernel, n_len, n_wid), out_shape=(pltpu....  23.7 us
    unnamed x2, local copies, waits for them, and re-layouts  2.29 us

profile of v3, /device:TPU:27, one launch (start us, length us, event | category | flops | bytes accessed | tf_op | source)
XLA Modules:
  0.0 26.6 jit_solution(14002795084016225552)
XLA Ops:
  0.6 23.7 %shard_map.68 = (f32[2,1024,256]{2,1,0:T(8,128)S(1)}, f32[1024,256]{1,0:T(8,128)S(1)}) custom-call(f32[2,1024,256]{2,1,0:T(8,128)} %bitcast.9, f32[1024,256]{1,0:T(8,128)} %bitcast.10, s32[1024,256]{1,0:T(8,128)} %bitcast.11, s32[1024,256]{1,0:T(8,128)} %bitcast.12, f32[1024,256]{1,0:T(8,128)} %bitcast.13), custom_call_target="tpu_custom_call" | custom-call | tf_op jit(solution)/shard_map/pallas_call | solution.py:509
  24.3 1.3 %copy.9 = f32[2,32,32,256]{3,2,1,0:T(8,128)} copy(f32[2,32,32,256]{3,2,1,0:T(8,128)S(1)} %bitcast.7) | data formatting | bytes 4194304
  25.7 1.0 %copy.10 = f32[32,32,256]{2,1,0:T(8,128)} copy(f32[32,32,256]{2,1,0:T(8,128)S(1)} %bitcast.8) | data formatting | bytes 2097152

commit v4 on v3

--- a/solution.py
+++ b/solution.py
@@ -105,7 +105,8 @@
         @pl.when(jnp.logical_not(has[0, dw]))
         def _():
             for h in range(2):
-                QR[side, h] = jnp.zeros((32, 128), jnp.float32)
+                for kind in range(2):
+                    QR[side, kind, h] = jnp.zeros((32, 128), jnp.float32)
                 for c in range(c0, c0 + 4):
                     for ref in (CT, KT, GT, E0T):
                         ref[side, c, h, pl.ds(TOWN, 32), :] = jnp.zeros((32, 128), jnp.float32)
@@ -132,9 +133,11 @@
     for side, col, c, sign in edges:
         for h in range(2):
             g = column(G, h, PAD, col)
-            CT[side, c, h, own_t, :] = conduct(column(MAT, h, 0, col))
+            cond = conduct(column(MAT, h, 0, col))
+            CT[side, c, h, own_t, :] = cond
             GT[side, c, h, own_t, :] = g
-            QS[side, h] = g - sign * (0.5 * (column(U0, h, 0, col) * column(B, h, 0, col)))
+            QS[side, 1, h] = cond
+            QS[side, 0, h] = g - sign * (0.5 * (column(U0, h, 0, col) * column(B, h, 0, col)))
     for copy in loads[8:]:
         copy.wait()
 
@@ -174,12 +177,12 @@
             def _():
                 copy.wait_recv()
 
-    def nat_part(ref, way, depth, here):
+    def nat_part(ref, way, depth, here, skip=0):
         if way[0] < 0:
-            first = NAT0 if here else NAT0 + 1024
+            first = (NAT0 if here else NAT0 + 1024) + 32 * skip
         else:
             first = NAT0 + 1024 - 32 * depth if here else NAT0 - 32 * depth
-        return ref.at[:, pl.ds(first, 32 * depth), :]
+        return ref.at[:, pl.ds(first, 32 * (depth - skip)), :]
 
     def strip_part(ref, way, near, far, here):
         count = far - near + 1
@@ -190,23 +193,22 @@
         if way[0] == 0:
             rows = own_t
         elif way[0] < 0:
-            rows = pl.ds(16 if here else 48, 4)
+            rows = pl.ds(16 if here else 48, far)
         else:
-            rows = pl.ds(44 if here else 12, 4)
+            rows = pl.ds((48 if here else 16) - far, far)
         return ref.at[side, pl.ds(first, count), :, rows, :]
 
     pl.semaphore_wait(barrier, sum(has[way].astype(jnp.int32) for way in straight))
 
     wid_ways, len_ways = straight[:2], straight[2:]
-    first_wid, first_len, later_len, later_wid = [], [], [], []
+    first_wid, first_len, later_len, later_wid, last = [], [], [], [], []
     for way in wid_ways:
         out, into = (0, 1) if way[1] < 0 else (1, 0)
         first_wid.append(message(way, QS.at[out], QR.at[into]))
-        first_wid.append(message(way, strip_part(CT, way, 1, 1, True), strip_part(CT, way, 1, 1, False)))
     for way in len_ways:
         Q = QM if way[0] < 0 else QP
         first_len.append(message(way, nat_part(Q, way, 1, True), nat_part(Q, way, 1, False)))
-        first_len.append(message(way, nat_part(C, way, 4, True), nat_part(C, way, 4, False)))
+        first_len.append(message(way, nat_part(C, way, 1, True), nat_part(C, way, 1, False)))
     for side in range(2):
         for col in OWN_COLS[side]:
             c = col - FIRST[side]
@@ -216,15 +218,6 @@
                     if 3 <= c <= 6:
                         GT[side, c, h, own_t, :] = column(G, h, PAD, col)
                 KT[side, c, h, own_t, :] = column(K, h, NAT0, col)
-    for way in wid_ways:
-        later_wid.append(message(way, strip_part(CT, way, 2, 4, True), strip_part(CT, way, 2, 4, False)))
-        later_wid.append(message(way, strip_part(KT, way, 1, 3, True), strip_part(KT, way, 1, 3, False)))
-        later_wid.append(message(way, strip_part(GT, way, 1, 1, True), strip_part(GT, way, 1, 1, False)))
-    for way in len_ways:
-        into = 1 if way[0] < 0 else 0
-        first = PAD if way[0] < 0 else PAD + 31 * 32
-        later_len.append(message(way, nat_part(K, way, 3, True), nat_part(K, way, 3, False)))
-        later_len.append(message(way, G.at[:, pl.ds(first, 32), :], GH.at[into]))
 
     shape = (32, 128)
     jj = lax.broadcasted_iota(jnp.int32, shape, 0)
@@ -283,7 +276,14 @@
         row(i)
         return carry
 
-    lax.fori_loop(1, 31, row_step, 0, unroll=5)
+    for way in wid_ways:
+        later_wid.append(message(way, strip_part(CT, way, 2, 4, True), strip_part(CT, way, 2, 4, False)))
+        later_wid.append(message(way, strip_part(KT, way, 1, 3, True), strip_part(KT, way, 1, 3, False)))
+    for way in len_ways:
+        later_len.append(message(way, nat_part(C, way, 4, True, 1), nat_part(C, way, 4, False, 1)))
+        later_len.append(message(way, nat_part(K, way, 3, True), nat_part(K, way, 3, False)))
+    lax.fori_loop(1, 11, row_step, 0, unroll=5)
+    lax.fori_loop(11, 31, row_step, 0, unroll=5)
 
     received(first_len)
     row(0)
@@ -306,9 +306,11 @@
     for side, col, c, sign in edges:
         halo = c - 1 if side == 0 else c + 1
         for h in range(2):
-            s = 0.5 * (CT[side, c, h, own_t, :] + CT[side, halo, h, own_t, :])
+            cond = QR[side, 1, h]
+            CT[side, halo, h, own_t, :] = cond
+            s = 0.5 * (CT[side, c, h, own_t, :] + cond)
             res = column(RP, h, 0, col) + s * (
-                QR[side, h] - sign * column(HW, h, PAD, col) - GT[side, c, h, own_t, :]
+                QR[side, 0, h] - sign * column(HW, h, PAD, col) - GT[side, c, h, own_t, :]
             )
             e = res / (column(DP, h, 0, col) + s)
             E0T[side, c, h, own_t, :] = e
@@ -319,6 +321,12 @@
         second.append(message(way, strip_part(E0T, way, 1, 3, True), strip_part(E0T, way, 1, 3, False)))
     for way in len_ways:
         second_len.append(message(way, nat_part(E0, way, 4, True), nat_part(E0, way, 4, False)))
+    for way in wid_ways:
+        last.append(message(way, strip_part(GT, way, 1, 1, True), strip_part(GT, way, 1, 1, False)))
+    for way in len_ways:
+        into = 1 if way[0] < 0 else 0
+        first = PAD if way[0] < 0 else PAD + 31 * 32
+        second_len.append(message(way, G.at[:, pl.ds(first, 32), :], GH.at[into]))
 
     E = (E0, E1, E2)
     ET = (E0T, E1T, E2T, E3T)
@@ -356,22 +364,9 @@
     sweep(2, 3, 28, 13)
 
     received(later_len)
-    received(later_wid)
     for i in (-3, -2, -1):
         row(i, has[-1, 0])
         row(31 - i, has[1, 0])
-    for side in range(2):
-        for col in OWN_COLS[side]:
-            c = col - FIRST[side]
-            for h in range(2):
-                CT[side, c, h, pl.ds(12, 4), :] = column(C, h, 0, col, 4)
-                CT[side, c, h, pl.ds(48, 4), :] = column(C, h, NAT0 + 1024, col, 4)
-                if 3 <= c <= 6:
-                    KT[side, c, h, pl.ds(13, 3), :] = column(K, h, 32, col, 3)
-                    KT[side, c, h, pl.ds(48, 3), :] = column(K, h, NAT0 + 1024, col, 3)
-                    GT[side, c, h, pl.ds(15, 1), :] = GH[0, h, pl.ds(col, 1), :]
-                    GT[side, c, h, pl.ds(48, 1), :] = GH[1, h, pl.ds(col, 1), :]
-
     received(second_len)
     for k in range(SWEEPS - 1):
         for i in (*range(k - 3, k + 1), *range(31 - k, 35 - k)):
@@ -387,6 +382,9 @@
             for h in range(2):
                 E0T[side, c, h, pl.ds(12, 4), :] = column(E0, h, 0, col, 4)
                 E0T[side, c, h, pl.ds(48, 4), :] = column(E0, h, NAT0 + 1024, col, 4)
+                if 3 <= c <= 6:
+                    GT[side, c, h, pl.ds(15, 1), :] = GH[0, h, pl.ds(col, 1), :]
+                    GT[side, c, h, pl.ds(48, 1), :] = GH[1, h, pl.ds(col, 1), :]
                 if col in (1, 2, 29, 30):
                     E1T[side, c, h, TAREA, :] = column(E1, h, 0, col, 40)
                 if col in (2, 3, 28, 29):
@@ -411,7 +409,18 @@
         lax.fori_loop(0, 32, step, 0, unroll=unroll)
 
     finish(8, 16, 4)
+    received(later_wid)
     received(later_diag)
+    for side in range(2):
+        for col in OWN_COLS[side]:
+            c = col - FIRST[side]
+            for h in range(2):
+                CT[side, c, h, pl.ds(12, 4), :] = column(C, h, 0, col, 4)
+                CT[side, c, h, pl.ds(48, 4), :] = column(C, h, NAT0 + 1024, col, 4)
+                if 3 <= c <= 6:
+                    KT[side, c, h, pl.ds(13, 3), :] = column(K, h, 32, col, 3)
+                    KT[side, c, h, pl.ds(48, 3), :] = column(K, h, NAT0 + 1024, col, 3)
+
 
     ii = lax.broadcasted_iota(jnp.int32, (40, 128), 0)
     rows_in = jnp.logical_and(
@@ -466,6 +475,7 @@
             for c in range(1 + k, 5 + k) if side == 0 else range(5 - k, 9 - k):
                 strip_sweep(c, 0)
 
+    received(last)
     for side in range(2):
         for c in range(3, 7):
             for h in range(2):
@@ -483,6 +493,18 @@
 
 
 N_MESSAGES = 36
+
+
+def deliver(vel, pot, vel_out, pot_out, sem):
+    copies = []
+    for half in range(2):
+        rows = pl.ds(512 * half, 512)
+        for src, dst in ((vel.at[0, rows], vel_out.at[0, rows]), (vel.at[1, rows], vel_out.at[1, rows]), (pot.at[rows], pot_out.at[rows])):
+            copies.append(pltpu.make_async_copy(src, dst, sem.at[len(copies)]))
+    for copy in copies:
+        copy.start()
+    for copy in copies:
+        copy.wait()
 
 
 def solution(mesh):
@@ -496,10 +518,11 @@
         strip = pltpu.VMEM((2, 10, 2, TROWS, 128), jnp.float32)
         ints = pltpu.VMEM((2, 1024, 128), jnp.int32)
         rows = pltpu.VMEM((2, 2, 32, 128), jnp.float32)
+        crit = pltpu.VMEM((2, 2, 2, 32, 128), jnp.float32)
         scratch = [
             own, own, own, ints, ints, padded, own, padded, nat, nat, nat, nat, own, own, nat, nat, nat,
             pltpu.VMEM((6, 2, 1024 + 2 * NAT0, 128), jnp.float32), rows,
-            strip, strip, strip, rows, rows, strip, strip, strip, strip,
+            strip, strip, strip, crit, crit, strip, strip, strip, strip,
             pltpu.VMEM((6, 2, 10, 2, TROWS, 128), jnp.float32),
             pltpu.VMEM((2, 40 * PW, 128), jnp.float32),
             pltpu.SemaphoreType.DMA((12,)),
@@ -519,6 +542,16 @@
                 collective_id=0, has_side_effects=True, vmem_limit_bytes=50 * 1024 * 1024
             ),
         )(flat(velocity), flat(bfield), flat(material), flat(wall_mask), flat(potential_guess))
+        vel, pot = pl.pallas_call(
+            deliver,
+            out_shape=(
+                jax.ShapeDtypeStruct((2, 1024, 256), jnp.float32),
+                jax.ShapeDtypeStruct((1024, 256), jnp.float32),
+            ),
+            in_specs=[pl.BlockSpec(memory_space=pltpu.VMEM)] * 2,
+            out_specs=(pl.BlockSpec(memory_space=pltpu.HBM), pl.BlockSpec(memory_space=pltpu.HBM)),
+            scratch_shapes=[pltpu.SemaphoreType.DMA((6,))],
+        )(*(pltpu.with_memory_space_constraint(a, pltpu.VMEM) for a in (vel, pot)))
         return vel.reshape(velocity.shape), pot.reshape(bfield.shape)
 
     whole, part = P(None, "len", "wid", None), P("len", "wid", None)

time: 26.7 us -> 25.4 us (0.951)
  local copies, waits for them, and re-layouts: 2.29 us -> 0 us
  Pallas kernels: 23.7 us -> 24.7 us
    unnamed x2 -> x0, local copies, waits for them, and re-layouts: 2.29 us -> none
    pallas_call x0 -> x1, Pallas kernels: none -> 1.71 us  [body(): pl.pallas_call(deliver, out_shape=(jax.ShapeDtypeStruct((2, 1024, 256), j...]
    pallas_call x1, Pallas kernels: 23.7 us -> 23 us  [body(): pl.pallas_call(functools.partial(kernel, n_len, n_wid), out_shape=(pltpu....]
where the time goes in v4:
time: 25.4 us; the launch traced here: 25.3 us
  Pallas kernels  24.7 us (97%)
  between operations  0.64 us (3%)
    pallas_call x1, Pallas kernels, body(): pl.pallas_call(functools.partial(kernel, n_len, n_wid), out_shape=(pltpu....  23 us
    pallas_call x1, Pallas kernels, body(): pl.pallas_call(deliver, out_shape=(jax.ShapeDtypeStruct((2, 1024, 256), j...  1.71 us

profile of v4, /device:TPU:27, one launch (start us, length us, event | category | flops | bytes accessed | tf_op | source)
XLA Modules:
  0.0 25.3 jit_solution(14629514943369547561)
XLA Ops:
  0.6 23.0 %shard_map.68 = (f32[2,1024,256]{2,1,0:T(8,128)S(1)}, f32[1024,256]{1,0:T(8,128)S(1)}) custom-call(f32[2,1024,256]{2,1,0:T(8,128)} %bitcast.7, f32[1024,256]{1,0:T(8,128)} %bitcast.8, s32[1024,256]{1,0:T(8,128)} %bitcast.9, s32[1024,256]{1,0:T(8,128)} %bitcast.10, f32[1024,256]{1,0:T(8,128)} %bitcast.11), custom_call_target="tpu_custom_call" | custom-call | tf_op jit(solution)/shard_map/pallas_call | solution.py:532
  23.6 1.7 %shard_map.69 = (f32[2,1024,256]{2,1,0:T(8,128)}, f32[1024,256]{1,0:T(8,128)}) custom-call(f32[2,1024,256]{2,1,0:T(8,128)S(1)} %get-tuple-element.6.vel, f32[1024,256]{1,0:T(8,128)S(1)} %get-tuple-element.7.pot), custom_call_target="tpu_custom_call" | custom-call | tf_op jit(solution)/shard_map/pallas_call | solution.py:545

commit v5 on v4

--- a/solution.py
+++ b/solution.py
@@ -62,9 +62,18 @@
     return [jnp.where(first, 0.0, r[0]) if zero else r[0], jnp.where(first, r[0], r[1])]
 
 
-def kernel(n_len, n_wid, u_hbm, b_hbm, m_hbm, w_hbm, g_hbm, vel_out, pot_out,
-           U0, U1, B, MAT, WALL, G, HL, HW, QP, QM, C, K, RP, DP, E0, E1, E2, TN, GH,
-           CT, KT, GT, QS, QR, E0T, E1T, E2T, E3T, TT, POT, lsem, ssem, rsem):
+def results(U0, U1, B, POT, h, i, first, count):
+    n = pl.multiple_of(32 * i + first, 8)
+    q = pl.multiple_of(PW * (i + DEEP) + 8 + first, 8)
+    at = (h, pl.ds(n, count), slice(None))
+    new_len = U0[at] - B[at] * (POT[h, pl.ds(q + 1, count), :] - POT[h, pl.ds(q - 1, count), :])
+    new_wid = U1[at] + B[at] * (POT[h, pl.ds(q + PW, count), :] - POT[h, pl.ds(q - PW, count), :])
+    return new_len, new_wid, POT[h, pl.ds(q, count), :]
+
+
+def kernel(n_len, n_wid, u_hbm, b_hbm, m_hbm, w_hbm, g_hbm, vel_out, pot_out, U0, U1, B, POT,
+           MAT, WALL, G, HL, HW, QP, QM, C, K, RP, DP, E0, E1, E2, TN, GH,
+           CT, KT, GT, QS, QR, E0T, E1T, E2T, E3T, TT, lsem, ssem, rsem):
     li, wi = lax.axis_index("len"), lax.axis_index("wid")
     has = {(-1, 0): li > 0, (1, 0): li < n_len - 1, (0, -1): wi > 0, (0, 1): wi < n_wid - 1}
     for dl in (-1, 1):
@@ -390,25 +399,17 @@
                 if col in (2, 3, 28, 29):
                     E2T[side, c, h, TAREA, :] = column(E2, h, 0, col, 40)
 
-    def finish(first, count, unroll):
-        def step(i, carry):
-            n = pl.multiple_of(32 * i + first, 8)
-            q = pl.multiple_of(PW * (i + DEEP) + 8 + first, 8)
-            for h in range(2):
-                at = (h, pl.ds(n, count), slice(None))
-                lanes = pl.ds(128 * h, 128)
-                pot_out[pl.ds(n, count), lanes] = POT[h, pl.ds(q, count), :]
-                vel_out[0, pl.ds(n, count), lanes] = U0[at] - B[at] * (
-                    POT[h, pl.ds(q + 1, count), :] - POT[h, pl.ds(q - 1, count), :]
-                )
-                vel_out[1, pl.ds(n, count), lanes] = U1[at] + B[at] * (
-                    POT[h, pl.ds(q + PW, count), :] - POT[h, pl.ds(q - PW, count), :]
-                )
-            return carry
-
-        lax.fori_loop(0, 32, step, 0, unroll=unroll)
-
-    finish(8, 16, 4)
+    def middle(i, carry):
+        n = pl.multiple_of(32 * i + 8, 8)
+        for h in range(2):
+            lanes = pl.ds(128 * h, 128)
+            new_len, new_wid, potential = results(U0, U1, B, POT, h, i, 8, 16)
+            vel_out[0, pl.ds(n, 16), lanes] = new_len
+            vel_out[1, pl.ds(n, 16), lanes] = new_wid
+            pot_out[pl.ds(n, 16), lanes] = potential
+        return carry
+
+    lax.fori_loop(0, 32, middle, 0, unroll=4)
     received(later_wid)
     received(later_diag)
     for side in range(2):
@@ -483,8 +484,6 @@
                 for k in range(SWEEPS):
                     total = total + GAINS[k] * ET[k][side, c, h, TAREA, :]
                 POT[h, pl.ds(8 + c + FIRST[side], 40, stride=PW), :] = total
-    finish(0, 8, 4)
-    finish(24, 8, 4)
 
     for way, copy in sent:
         @pl.when(has[way])
@@ -495,14 +494,31 @@
 N_MESSAGES = 36
 
 
-def deliver(vel, pot, vel_out, pot_out, sem):
+def deliver(vel, pot, U0, U1, B, POT, vel_out, pot_out, outer, sem):
     copies = []
-    for half in range(2):
-        rows = pl.ds(512 * half, 512)
-        for src, dst in ((vel.at[0, rows], vel_out.at[0, rows]), (vel.at[1, rows], vel_out.at[1, rows]), (pot.at[rows], pot_out.at[rows])):
-            copies.append(pltpu.make_async_copy(src, dst, sem.at[len(copies)]))
-    for copy in copies:
-        copy.start()
+
+    def out(src, dst):
+        copies.append(pltpu.make_async_copy(src, dst, sem.at[len(copies)]))
+        copies[-1].start()
+
+    inner = pl.ds(8, 16)
+    for part in range(2):
+        out(vel.at[part, :, inner], vel_out.at[part, :, inner])
+    out(pot.at[:, inner], pot_out.at[:, inner])
+    for side in range(2):
+        first = 24 * side
+
+        def step(i, carry):
+            for h in range(2):
+                lanes = pl.ds(128 * h, 128)
+                for part, value in enumerate(results(U0, U1, B, POT, h, i, first, 8)):
+                    outer[side, part, i, :, lanes] = value
+            return carry
+
+        lax.fori_loop(0, 32, step, 0, unroll=8)
+        for part in range(2):
+            out(outer.at[side, part], vel_out.at[part, :, pl.ds(first, 8)])
+        out(outer.at[side, 2], pot_out.at[:, pl.ds(first, 8)])
     for copy in copies:
         copy.wait()
 
@@ -520,39 +536,43 @@
         rows = pltpu.VMEM((2, 2, 32, 128), jnp.float32)
         crit = pltpu.VMEM((2, 2, 2, 32, 128), jnp.float32)
         scratch = [
-            own, own, own, ints, ints, padded, own, padded, nat, nat, nat, nat, own, own, nat, nat, nat,
+            ints, ints, padded, own, padded, nat, nat, nat, nat, own, own, nat, nat, nat,
             pltpu.VMEM((6, 2, 1024 + 2 * NAT0, 128), jnp.float32), rows,
             strip, strip, strip, crit, crit, strip, strip, strip, strip,
             pltpu.VMEM((6, 2, 10, 2, TROWS, 128), jnp.float32),
-            pltpu.VMEM((2, 40 * PW, 128), jnp.float32),
             pltpu.SemaphoreType.DMA((12,)),
             pltpu.SemaphoreType.DMA((N_MESSAGES,)),
             pltpu.SemaphoreType.DMA((N_MESSAGES,)),
         ]
-        vel, pot = pl.pallas_call(
+        kept = pl.pallas_call(
             functools.partial(kernel, n_len, n_wid),
             out_shape=(
                 pltpu.VMEM((2, 1024, 256), jnp.float32),
                 pltpu.VMEM((1024, 256), jnp.float32),
+                own,
+                own,
+                own,
+                pltpu.VMEM((2, 40 * PW, 128), jnp.float32),
             ),
             in_specs=[pl.BlockSpec(memory_space=pltpu.HBM)] * 5,
-            out_specs=(pl.BlockSpec(memory_space=pltpu.VMEM), pl.BlockSpec(memory_space=pltpu.VMEM)),
+            out_specs=(pl.BlockSpec(memory_space=pltpu.VMEM),) * 6,
             scratch_shapes=scratch,
             compiler_params=pltpu.CompilerParams(
-                collective_id=0, has_side_effects=True, vmem_limit_bytes=50 * 1024 * 1024
+                collective_id=0, has_side_effects=True, vmem_limit_bytes=45 * 1024 * 1024
             ),
         )(flat(velocity), flat(bfield), flat(material), flat(wall_mask), flat(potential_guess))
-        vel, pot = pl.pallas_call(
+        kept = (kept[0].reshape(2, 32, 32, 256), kept[1].reshape(32, 32, 256)) + tuple(kept[2:])
+        return pl.pallas_call(
             deliver,
             out_shape=(
-                jax.ShapeDtypeStruct((2, 1024, 256), jnp.float32),
-                jax.ShapeDtypeStruct((1024, 256), jnp.float32),
+                jax.ShapeDtypeStruct((2, 32, 32, 256), jnp.float32),
+                jax.ShapeDtypeStruct((32, 32, 256), jnp.float32),
             ),
-            in_specs=[pl.BlockSpec(memory_space=pltpu.VMEM)] * 2,
+            in_specs=[pl.BlockSpec(memory_space=pltpu.VMEM)] * 6,
             out_specs=(pl.BlockSpec(memory_space=pltpu.HBM), pl.BlockSpec(memory_space=pltpu.HBM)),
-            scratch_shapes=[pltpu.SemaphoreType.DMA((6,))],
-        )(*(pltpu.with_memory_space_constraint(a, pltpu.VMEM) for a in (vel, pot)))
-        return vel.reshape(velocity.shape), pot.reshape(bfield.shape)
+            scratch_shapes=[pltpu.VMEM((2, 3, 32, 8, 256), jnp.float32), pltpu.SemaphoreType.DMA((9,))],
+            compiler_params=pltpu.CompilerParams(vmem_limit_bytes=8 * 1024 * 1024),
+        )(*(pltpu.with_memory_space_constraint(a, pltpu.VMEM) for a in kept))
 
     whole, part = P(None, "len", "wid", None), P("len", "wid", None)
     return jax.shard_map(

time: 25.4 us -> 25 us (0.984)
  Pallas kernels: 24.7 us -> 24.3 us
    pallas_call x1, Pallas kernels: 23 us -> 22.6 us  [body(): pl.pallas_call(functools.partial(kernel, n_len, n_wid), out_shape=(pltpu....]
where the time goes in v5:
time: 25 us
  Pallas kernels  24.3 us (97%)
  between operations  0.64 us (3%)
    pallas_call x1, Pallas kernels, body(): pl.pallas_call(functools.partial(kernel, n_len, n_wid), out_shape=(pltpu....  22.6 us
    pallas_call x1, Pallas kernels, body(): pl.pallas_call(deliver, out_shape=(jax.ShapeDtypeStruct((2, 32, 32, 256),...  1.73 us

profile of v5, /device:TPU:27, one launch (start us, length us, event | category | flops | bytes accessed | tf_op | source)
XLA Modules:
  0.0 25.0 jit_solution(8130386973586197301)
XLA Ops:
  0.6 22.6 %shard_map.68 = (f32[2,1024,256]{2,1,0:T(8,128)S(1)}, f32[1024,256]{1,0:T(8,128)S(1)}, f32[2,1024,128]{2,1,0:T(8,128)S(1)}, f32[2,1024,128]{2,1,0:T(8,128)S(1)},...) custom-call(f32[2,1024,256]{2,1,0:T(8,128)} %bitcast.9, f32[1024,256]{1,0:T(8,128)} %bitcast.10, ...), custom_call_target="tpu_custom_call" | custom-call | tf_op jit(solution)/shard_map/pallas_call | solution.py:547
  23.2 1.7 %shard_map.69 = (f32[2,32,32,256]{3,2,1,0:T(8,128)}, f32[32,32,256]{2,1,0:T(8,128)}) custom-call(f32[2,32,32,256]{3,2,1,0:T(8,128)S(1)} %bitcast.7, f32[32,32,256]{2,1,0:T(8,128)S(1)} %bitcast.8, f32[2,1024,128]{2,1,0:T(8,128)S(1)} %get-tuple-element.10.U0, f32[2,1024,128]{2,1,0:T(8,128)S(1)} %get-tuple-element.11.U1, ...), custom_call_target="tpu_custom_call" | custom-call | tf_op jit(solution)/shard_map/pallas_call | solution.py:565

commit v6 on v5

--- a/solution.py
+++ b/solution.py
@@ -165,7 +165,8 @@
             QM[h, pl.ds(o, 32), :] = g - hl
         return carry
 
-    lax.fori_loop(0, 32, prepare, 0, unroll=4)
+    prepare(0, 0)
+    prepare(31, 0)
 
     sent = []
 
@@ -218,6 +219,7 @@
         Q = QM if way[0] < 0 else QP
         first_len.append(message(way, nat_part(Q, way, 1, True), nat_part(Q, way, 1, False)))
         first_len.append(message(way, nat_part(C, way, 1, True), nat_part(C, way, 1, False)))
+    lax.fori_loop(1, 31, prepare, 0, unroll=5)
     for side in range(2):
         for col in OWN_COLS[side]:
             c = col - FIRST[side]
@@ -324,10 +326,10 @@
             e = res / (column(DP, h, 0, col) + s)
             E0T[side, c, h, own_t, :] = e
             E0[h, pl.ds(NAT0 + col, 32, stride=32), :] = e
+    for way in diagonal:
+        second.append(message(way, strip_part(E0T, way, 1, 3, True), strip_part(E0T, way, 1, 3, False)))
     for way in wid_ways:
         second.append(message(way, strip_part(E0T, way, 1, 1, True), strip_part(E0T, way, 1, 1, False)))
-    for way in diagonal:
-        second.append(message(way, strip_part(E0T, way, 1, 3, True), strip_part(E0T, way, 1, 3, False)))
     for way in len_ways:
         second_len.append(message(way, nat_part(E0, way, 4, True), nat_part(E0, way, 4, False)))
     for way in wid_ways:

time: 25 us -> 24.4 us (0.976)
  Pallas kernels: 24.3 us -> 23.7 us
    pallas_call x1, Pallas kernels: 22.6 us -> 22 us  [body(): pl.pallas_call(functools.partial(kernel, n_len, n_wid), out_shape=(pltpu....]
where the time goes in v6:
time: 24.4 us
  Pallas kernels  23.7 us (97%)
  between operations  0.64 us (3%)
    pallas_call x1, Pallas kernels, body(): pl.pallas_call(functools.partial(kernel, n_len, n_wid), out_shape=(pltpu....  22 us
    pallas_call x1, Pallas kernels, body(): pl.pallas_call(deliver, out_shape=(jax.ShapeDtypeStruct((2, 32, 32, 256),...  1.73 us

profile of v6, /device:TPU:27, one launch (start us, length us, event | category | flops | bytes accessed | tf_op | source)
XLA Modules:
  0.0 24.4 jit_solution(7712074878291523643)
XLA Ops:
  0.6 22.0 %shard_map.68 = (f32[2,1024,256]{2,1,0:T(8,128)S(1)}, f32[1024,256]{1,0:T(8,128)S(1)}, f32[2,1024,128]{2,1,0:T(8,128)S(1)}, f32[2,1024,128]{2,1,0:T(8,128)S(1)},...) custom-call(f32[2,1024,256]{2,1,0:T(8,128)} %bitcast.9, f32[1024,256]{1,0:T(8,128)} %bitcast.10, ...), custom_call_target="tpu_custom_call" | custom-call | tf_op jit(solution)/shard_map/pallas_call | solution.py:549
  22.6 1.7 %shard_map.69 = (f32[2,32,32,256]{3,2,1,0:T(8,128)}, f32[32,32,256]{2,1,0:T(8,128)}) custom-call(f32[2,32,32,256]{3,2,1,0:T(8,128)S(1)} %bitcast.7, f32[32,32,256]{2,1,0:T(8,128)S(1)} %bitcast.8, f32[2,1024,128]{2,1,0:T(8,128)S(1)} %get-tuple-element.10.U0, f32[2,1024,128]{2,1,0:T(8,128)S(1)} %get-tuple-element.11.U1, ...), custom_call_target="tpu_custom_call" | custom-call | tf_op jit(solution)/shard_map/pallas_call | solution.py:567
